TPU v7x, 256 devices: a whole 4x4x8 slice. The times are simulated.
256 devices in a mesh: slide: 8 (over x, y_hi), tile: 32 (over y_lo, z, core).
Axes of the slice: x: 4, y: 4 (y_hi: 2, y_lo: 2; y = y_hi * 2 + y_lo), z: 8, core: 2. Of those that a mesh axis runs over, the one named last changes fastest.
Arguments:
- slide_tiles: bfloat16 [8, 1024, 16, 16, 256], P('slide', 'tile'), may hold values from -6 to 6
- balance_list: int32 [8, 1024], P('slide'), may hold values from -1 to 575, as said below
- output_grad: bfloat16 [8, 1024, 8, 8, 512], P('slide', 'tile'), may hold values from -6 to 6
- w_reduce: bfloat16 [256, 128], replicated, may hold values from -0.375 to 0.375
- w_spatial: bfloat16 [1152, 128], replicated, may hold values from -0.1875 to 0.1875
- w_expand: bfloat16 [128, 512], replicated, may hold values from -0.5 to 0.5
- w_shortcut: bfloat16 [256, 512], replicated, may hold values from -0.375 to 0.375
Outputs:
- input_grad: bfloat16 [8, 1024, 16, 16, 256], P('slide', 'tile')
- grad_reduce: float32 [256, 128], replicated
- grad_spatial: float32 [1152, 128], replicated
- grad_expand: float32 [128, 512], replicated
- grad_shortcut: float32 [256, 512], replicated
Inputs may be any that keep to these rules, and one draw needn't show every extreme that they name: `balance_list`: block b of a slide belongs to grid row b // 32. Entry w * 18 + s says that device w of the tile axis computes the block as its s-th; every value from 0 to 575 appears exactly once in each slide, the rest are -1. The blocks of one grid row that go to one device are at most 1, and some row sends exactly 1 to a device in every slide.
All inputs are finite; a program needn't handle non-finite values.
Results may differ from a plain program's by a relative error of at most 0.0066.
Values may be sent and summed in bfloat16 or wider, within the bound.
A program may use at most 128 MiB of HBM per device.

v0:
```python
import jax
import jax.numpy as jnp
from jax import lax
from jax.sharding import PartitionSpec as P

WORK = 18


def slope_silu(value):
    sig = jax.nn.sigmoid(value)
    return sig * (1.0 + value * (1.0 - sig))


def select_rows(table, index):
    safe = jnp.maximum(index, 0)
    taken = jnp.take(table, safe, axis=0)
    keep = (index >= 0).reshape((-1,) + (1,) * (table.ndim - 1))
    return jnp.where(keep, taken, jnp.zeros((), table.dtype))


def invert_slots(index, count):
    match = index[None, :] == jnp.arange(count, dtype=jnp.int32)[:, None]
    source = jnp.sum(
        jnp.where(match, jnp.arange(index.shape[0], dtype=jnp.int32)[None, :], 0), axis=1
    )
    return jnp.where(jnp.any(match, axis=1), source, -1)


def lookup_small(table, index):
    match = jnp.arange(table.shape[0], dtype=jnp.int32)[None, :] == index[:, None]
    return jnp.sum(jnp.where(match, table[None, :], 0), axis=1)


def body(slide_tiles, balance_list, output_grad, w_reduce, w_spatial, w_expand, w_shortcut):
    groups = lax.axis_size("tile")
    device = lax.axis_index("tile")
    blocks = slide_tiles[0]
    own_cols = blocks.shape[0]
    block_side = blocks.shape[1]
    half_side = block_side // 2
    chan_mid = w_reduce.shape[1]
    slot_cap = -(-own_cols // groups)
    slot_count = groups * slot_cap
    flat_place = balance_list[0]
    layout = flat_place.reshape(groups, own_cols)
    tissue = layout >= 0
    worker_of = jnp.where(tissue, layout // WORK, -1)
    col_index = jnp.arange(own_cols, dtype=jnp.int32)
    earlier = (worker_of[:, :, None] == worker_of[:, None, :]) & (
        col_index[None, None, :] < col_index[None, :, None]
    )
    rank = jnp.sum(earlier.astype(jnp.int32), axis=2)
    position = jnp.where(tissue, worker_of * slot_cap + rank, -1)
    my_position = lax.dynamic_index_in_dim(position, device, 0, keepdims=False)
    block_ids = invert_slots(flat_place, groups * WORK)
    block_ids = lax.dynamic_slice_in_dim(block_ids, device * WORK, WORK)
    grid_row = block_ids // own_cols
    grid_col = block_ids % own_cols
    slot_position = grid_row * slot_cap + lookup_small(rank.reshape(-1), block_ids)
    back_source = invert_slots(slot_position, slot_count)
    send_source = invert_slots(my_position, slot_count)

    def neighbour(row_step, col_step):
        new_row = grid_row + row_step
        new_col = grid_col + col_step
        inside = (new_row >= 0) & (new_row < groups) & (new_col >= 0) & (new_col < own_cols)
        found = lookup_small(flat_place, new_row * own_cols + new_col)
        return jnp.where(inside & (found >= 0), found, -1)

    received = (
        lax.all_to_all(
            select_rows(blocks, send_source), "tile", split_axis=0, concat_axis=0, tiled=True
        ),
        lax.all_to_all(
            select_rows(output_grad[0], send_source),
            "tile",
            split_axis=0,
            concat_axis=0,
            tiled=True,
        ),
    )
    work_in = select_rows(received[0], slot_position)
    work_grad = select_rows(received[1], slot_position)
    row_mask = jnp.ones((WORK, 1, 1, 1), bool)
    count = WORK
    pre = jnp.einsum("bhwc,cd->bhwd", work_in, w_reduce, preferred_element_type=jnp.float32)
    hidden = jax.nn.silu(pre).astype(jnp.bfloat16)
    published = jnp.concatenate([hidden[:, block_side - 1], hidden[:, :, block_side - 1]], axis=1)
    rim_table = lax.all_gather(published, "tile", axis=0, tiled=True)
    up_row = select_rows(rim_table, neighbour(-1, 0))[:, :block_side]
    left_col = select_rows(rim_table, neighbour(0, -1))[:, block_side:]
    corner = select_rows(rim_table, neighbour(-1, -1))[:, block_side - 1]
    top_line = jnp.concatenate([corner[:, None], up_row], axis=1)
    inner = jnp.concatenate([left_col[:, :, None], hidden], axis=2)
    extended = jnp.concatenate([top_line[:, None], inner], axis=1)
    span = 2 * half_side
    patches = jnp.concatenate(
        [
            extended[:, row_tap : row_tap + span : 2, col_tap : col_tap + span : 2]
            for row_tap in range(3)
            for col_tap in range(3)
        ],
        axis=-1,
    )
    act = jnp.einsum("bhwk,kd->bhwd", patches, w_spatial, preferred_element_type=jnp.float32)
    gated = jax.nn.silu(act).astype(jnp.bfloat16)
    skip_in = work_in[:, ::2, ::2]
    total = jnp.einsum(
        "bhwc,cd->bhwd", gated, w_expand, preferred_element_type=jnp.float32
    ) + jnp.einsum("bhwc,cd->bhwd", skip_in, w_shortcut, preferred_element_type=jnp.float32)
    grad_total = (work_grad.astype(jnp.float32) * slope_silu(total)).astype(jnp.bfloat16)
    grad_expand = jnp.einsum("bhwc,bhwd->cd", gated, grad_total, preferred_element_type=jnp.float32)
    grad_shortcut = jnp.einsum(
        "bhwc,bhwd->cd", skip_in, grad_total, preferred_element_type=jnp.float32
    )
    grad_gated = jnp.einsum(
        "bhwd,cd->bhwc", grad_total, w_expand, preferred_element_type=jnp.float32
    )
    grad_act = (grad_gated * slope_silu(act)).astype(jnp.bfloat16)
    grad_spatial = jnp.einsum(
        "bhwk,bhwd->kd", patches, grad_act, preferred_element_type=jnp.float32
    )
    grad_patch = jnp.einsum(
        "bhwd,kd->bhwk", grad_act, w_spatial, preferred_element_type=jnp.float32
    )
    grad_ext = jnp.zeros((count, block_side + 1, block_side + 1, chan_mid), jnp.float32)
    for row_tap in range(3):
        for col_tap in range(3):
            tap = row_tap * 3 + col_tap
            grad_ext = grad_ext.at[
                :, row_tap : row_tap + span : 2, col_tap : col_tap + span : 2
            ].add(grad_patch[..., tap * chan_mid : (tap + 1) * chan_mid])
    grad_hidden = grad_ext[:, 1:, 1:]
    outgoing = jnp.concatenate(
        [grad_ext[:, 0, 1:], grad_ext[:, 1:, 0], grad_ext[:, 0, 0][:, None]], axis=1
    )
    grad_table = lax.all_gather(outgoing.astype(jnp.bfloat16), "tile", axis=0, tiled=True).astype(
        outgoing.dtype
    )
    bottom_add = select_rows(grad_table, neighbour(1, 0))[:, :block_side]
    right_add = select_rows(grad_table, neighbour(0, 1))[:, block_side : 2 * block_side]
    diagonal = select_rows(grad_table, neighbour(1, 1))[:, 2 * block_side]
    bottom_add = bottom_add.at[:, block_side - 1].add(diagonal)
    grad_hidden = grad_hidden.at[:, block_side - 1, :].add(bottom_add)
    grad_hidden = grad_hidden.at[:, :, block_side - 1].add(right_add)
    grad_pre = jnp.where(row_mask, grad_hidden * slope_silu(pre), 0.0).astype(jnp.bfloat16)
    grad_reduce = jnp.einsum("bhwc,bhwd->cd", work_in, grad_pre, preferred_element_type=jnp.float32)
    grad_input = jnp.einsum("bhwd,cd->bhwc", grad_pre, w_reduce, preferred_element_type=jnp.float32)
    grad_input = grad_input.at[:, ::2, ::2].add(
        jnp.einsum("bhwd,cd->bhwc", grad_total, w_shortcut, preferred_element_type=jnp.float32)
    )
    grad_input = grad_input.astype(jnp.bfloat16)
    returned = lax.all_to_all(
        select_rows(grad_input, back_source), "tile", split_axis=0, concat_axis=0, tiled=True
    )
    input_grad = select_rows(returned, my_position)[None]
    summed = lax.psum((grad_reduce, grad_spatial, grad_expand, grad_shortcut), ("slide", "tile"))
    return (input_grad, summed[0], summed[1], summed[2], summed[3])


def solution(mesh):
    in_specs = (
        P("slide", "tile", None, None, None),
        P("slide", None),
        P("slide", "tile", None, None, None),
        P(),
        P(),
        P(),
        P(),
    )
    out_specs = (P("slide", "tile", None, None, None), P(), P(), P(), P())
    return jax.shard_map(body, mesh=mesh, in_specs=in_specs, out_specs=out_specs, check_vma=False)
```

profile of v0, /device:TPU:1, one launch (start us, length us, event | category | flops | bytes accessed | tf_op | source)
XLA Modules:
  0.0 1126.1 jit_solution(11346137806228832098)
XLA Ops:
  16.0 5.0 gather_fusion.4
  21.0 4.7 select_select_fusion.1
  25.8 11.2 all-to-all-start.1
  37.1 94.6 %all-to-all-done.1 = bf16[32,16,16,256]{3,2,1,0:T(8,128)(2,1)} async-done(((bf16[32,16,16,256]{3,2,1,0:T(8,128)(2,1)}), bf16[32,16,16,256]{3,2,1,0:T(8,128)(2,1)}, u32[]{:S(2)}, u32[]{:S(2)}) %all-to-all-start.1) | async-done | bytes 4194336 | tf_op jit(solution)/shard_map/all_to_all | solution.py:71
  131.6 4.5 gather_fusion.2
  138.2 2.2 multiply_convert_fusion.2
  143.3 3.3 select_select_fusion.4
  146.6 7.2 all-to-all-start
  161.0 57.1 %all-to-all-done = bf16[32,8,8,512]{3,2,1,0:T(8,128)(2,1)S(1)} async-done(((bf16[32,8,8,512]{3,2,1,0:T(8,128)(2,1)}), bf16[32,8,8,512]{3,2,1,0:T(8,128)(2,1)S(1)}, u32[]{:S(2)}, u32[]{:S(2)}) %all-to-all-start) | async-done | bytes 2097184 | tf_op jit(solution)/shard_map/all_to_all | solution.py:74
  219.9 64.7 %slice.188 = bf16[18,8,8,256]{3,2,1,0:T(8,128)(2,1)} slice(bf16[18,16,16,256]{3,2,1,0:T(8,128)(2,1)} %copy-done.3), slice={[0:18:1], [0:16:2], [0:16:2], [0:256:1]} | slice | bytes 1179648 | tf_op jit(solution)/shard_map/slice | solution.py:107
  284.6 42.6 %slice.187 = bf16[18,8,8,128]{3,2,1,0:T(8,128)(2,1)} slice(bf16[18,16,16,128]{3,2,1,0:T(8,128)(2,1)S(1)} %get-tuple-element.122), slice={[0:18:1], [1:16:2], [1:16:2], [0:128:1]} | slice | bytes 589824 | tf_op jit(solution)/shard_map/slice | solution.py:99
  327.1 42.7 %slice.186 = bf16[18,8,8,128]{3,2,1,0:T(8,128)(2,1)} slice(bf16[18,16,16,128]{3,2,1,0:T(8,128)(2,1)S(1)} %get-tuple-element.122), slice={[0:18:1], [1:16:2], [0:16:2], [0:128:1]} | slice | bytes 589824 | tf_op jit(solution)/shard_map/slice | solution.py:99
  369.8 42.5 %slice.184 = bf16[18,8,8,128]{3,2,1,0:T(8,128)(2,1)} slice(bf16[18,16,16,128]{3,2,1,0:T(8,128)(2,1)S(1)} %get-tuple-element.122), slice={[0:18:1], [0:16:2], [1:16:2], [0:128:1]} | slice | bytes 589824 | tf_op jit(solution)/shard_map/slice | solution.py:99
  412.3 42.6 %slice.183 = bf16[18,8,8,128]{3,2,1,0:T(8,128)(2,1)} slice(bf16[18,16,16,128]{3,2,1,0:T(8,128)(2,1)S(1)} %get-tuple-element.122), slice={[0:18:1], [0:16:2], [0:16:2], [0:128:1]} | slice | bytes 589824 | tf_op jit(solution)/shard_map/slice | solution.py:99
  454.9 2.9 gather_fusion.7
  458.0 2.9 gather_fusion.5
  461.0 2.9 gather_fusion.6
  464.9 42.7 %slice.181 = bf16[18,8,8,128]{3,2,1,0:T(8,128)(2,1)} slice(bf16[18,17,17,128]{3,2,1,0:T(8,128)(2,1)S(1)} %maximum_maximum_fusion), slice={[0:18:1], [0:16:2], [2:17:2], [0:128:1]} | slice | bytes 589824 | tf_op jit(solution)/shard_map/slice | solution.py:99
  507.5 42.6 %slice.180 = bf16[18,8,8,128]{3,2,1,0:T(8,128)(2,1)} slice(bf16[18,17,17,128]{3,2,1,0:T(8,128)(2,1)S(1)} %maximum_maximum_fusion), slice={[0:18:1], [0:16:2], [1:17:2], [0:128:1]} | slice | bytes 589824 | tf_op jit(solution)/shard_map/slice | solution.py:99
  550.1 42.2 %slice.179 = bf16[18,8,8,128]{3,2,1,0:T(8,128)(2,1)} slice(bf16[18,17,17,128]{3,2,1,0:T(8,128)(2,1)S(1)} %maximum_maximum_fusion), slice={[0:18:1], [0:16:2], [0:16:2], [0:128:1]} | slice | bytes 589824 | tf_op jit(solution)/shard_map/slice | solution.py:99
  593.2 3.1 slice.182
  596.2 5.1 slice.185
  623.1 6.2 scatter_fusion
  629.3 6.4 scatter_fusion.1
  635.7 6.2 scatter_fusion.2
  641.9 6.2 scatter_fusion.3
  648.1 6.2 scatter_fusion.4
  654.3 6.2 scatter_fusion.5
  660.5 6.2 scatter_fusion.6
  666.7 6.2 scatter_fusion.7
  672.9 6.1 scatter_fusion.8
  692.4 60.1 %all-gather.5.cloned.1.call-done = bf16[576,33,128]{2,1,0:T(8,128)(2,1)} async-done(((bf16[18,33,128]{2,1,0:T(8,128)(2,1)}), bf16[576,33,128]{2,1,0:T(8,128)(2,1)}) %all-gather.5.cloned.1.call-update) | async-done | bytes 4866064 | tf_op jit(solution)/shard_map/all_gather | solution.py:137
  752.4 7.8 convert_element_type.34
  760.3 5.8 gather_fusion.10
  766.1 5.8 gather_fusion.9
  771.9 5.0 gather_fusion.8
  779.5 7.1 scatter-add.96
  786.5 2.6 multiply_convert_fusion
  789.1 3.8 fusion.2
  792.9 9.2 scatter_fusion.9
  802.1 4.1 copy.142
  806.2 3.0 gather_fusion.3
  809.2 4.7 select_select_fusion.2
  813.9 6.6 all-to-all-start.2
  827.1 92.1 %all-to-all-done.2 = bf16[32,16,16,256]{3,2,1,0:T(8,128)(2,1)} async-done(((bf16[32,16,16,256]{3,2,1,0:T(8,128)(2,1)}), bf16[32,16,16,256]{3,2,1,0:T(8,128)(2,1)}, u32[]{:S(2)}, u32[]{:S(2)}) %all-to-all-start.2) | async-done | bytes 4194336 | tf_op jit(solution)/shard_map/all_to_all | solution.py:153
  919.2 5.0 gather_fusion.11
  924.3 4.9 fusion
  929.1 183.2 %all-reduce.3.cloned.1.call-done = (f32[256,128]{1,0:T(8,128)}, f32[1152,128]{1,0:T(8,128)}, f32[128,512]{1,0:T(8,128)}, f32[256,512]{1,0:T(8,128)}) async-done(((f32[256,128]{1,0:T(8,128)}, f32[1152,128]{1,0:T(8,128)}, f32[128,512]{1,0:T(8,128)}, f32[256,512]{1,0:T(8,128)}), (f32[256,128]{1,0:T(8,128)}, f32[1152,128]{1,0:T(8,128)}, f32[128,512]{1,0:T(8,128)}, ...) | async-done | bytes 1507344 | tf_op jit(solution)/shard_map/psum | solution.py:157
  (221 shorter events, 75.4 us)
Async XLA Ops:
  7.2 134.1 %copy-start = (bf16[1,32,8,8,512]{4,3,2,1,0:T(8,128)(2,1)S(1)}, bf16[1,32,8,8,512]{4,3,2,1,0:T(8,128)(2,1)}, u32[]{:S(2)}) copy-start(bf16[1,32,8,8,512]{4,3,2,1,0:T(8,128)(2,1)} %param.21) | copy-start | bytes 6291460
  12.5 8.5 copy-start.41
  25.8 105.9 %all-to-all-start.1 = ((bf16[32,16,16,256]{3,2,1,0:T(8,128)(2,1)}), bf16[32,16,16,256]{3,2,1,0:T(8,128)(2,1)}, u32[]{:S(2)}, u32[]{:S(2)}) async-start(bf16[32,16,16,256]{3,2,1,0:T(8,128)(2,1)} %select_select_fusion.1), calls=%async_computation.1 | async-start | bytes 8388608 | tf_op jit(solution)/shard_map/all_to_all | solution.py:71
  37.0 417.9 %all-gather.3.cloned.1.call-start = ((), (), s32[]{:S(2)}) async-start(), calls=%async_computation.3 | async-start | bytes 4866048 | tf_op jit(solution)/shard_map/all_gather | solution.py:89
  37.1 99.0 %copy-start.38 = (pred[18]{0:T(512)(128)(4,1)}, pred[18]{0:T(512)(128)(4,1)S(1)}, u32[]{:S(2)}) copy-start(pred[18]{0:T(512)(128)(4,1)S(1)} %broadcast_compare_fusion.9) | copy-start | bytes 58
  136.1 2.0 copy-start.27
  138.2 2.2 copy-start.3
  146.6 71.5 %all-to-all-start = ((bf16[32,8,8,512]{3,2,1,0:T(8,128)(2,1)}), bf16[32,8,8,512]{3,2,1,0:T(8,128)(2,1)S(1)}, u32[]{:S(2)}, u32[]{:S(2)}) async-start(bf16[32,8,8,512]{3,2,1,0:T(8,128)(2,1)} %select_select_fusion.4), calls=%async_computation | async-start | bytes 4194304 | tf_op jit(solution)/shard_map/all_to_all | solution.py:74
  153.8 598.6 %all-gather.5.cloned.1.call-start = ((), (), s32[]{:S(2)}) async-start(), calls=%async_computation.4 | async-start | bytes 6082560 | tf_op jit(solution)/shard_map/all_gather | solution.py:137
  593.1 10.4 copy-start.18
  593.1 10.6 copy-start.17
  593.2 10.6 copy-start.16
  596.2 7.7 copy-start.15
  601.4 2.7 copy-start.14
  602.4 1.7 copy-start.9
  604.0 1.1 copy-start.26
  604.2 1.5 copy-start.5
  605.0 3.1 copy-start.7
  605.0 1.5 copy-start.10
  605.1 1.6 copy-start.20
  605.1 1.7 copy-start.24
  605.1 1.7 copy-start.39
  608.2 1.1 copy-start.11
  679.0 1.1 copy-start.35
  688.2 1.3 copy-start.12
  688.2 1.3 copy-start.25
  692.3 84.6 %copy-start.36 = (pred[18]{0:T(512)(128)(4,1)S(1)}, pred[18]{0:T(512)(128)(4,1)}, u32[]{:S(2)}) copy-start(pred[18]{0:T(512)(128)(4,1)} %get-tuple-element.99) | copy-start | bytes 58
  692.3 84.6 %copy-start.37 = (pred[18]{0:T(512)(128)(4,1)S(1)}, pred[18]{0:T(512)(128)(4,1)}, u32[]{:S(2)}) copy-start(pred[18]{0:T(512)(128)(4,1)} %get-tuple-element.129) | copy-start | bytes 58
  760.3 16.8 %copy-start.32 = (pred[18]{0:T(512)(128)(4,1)S(1)}, pred[18]{0:T(512)(128)(4,1)}, u32[]{:S(2)}) copy-start(pred[18]{0:T(512)(128)(4,1)} %get-tuple-element.65) | copy-start | bytes 58
  760.3 16.8 %copy-start.40 = (pred[18]{0:T(512)(128)(4,1)S(1)}, pred[18]{0:T(512)(128)(4,1)}, u32[]{:S(2)}) copy-start(pred[18]{0:T(512)(128)(4,1)} %broadcast_compare_fusion.14) | copy-start | bytes 58
  760.3 17.9 %copy-start.31 = (pred[18]{0:T(512)(128)(4,1)S(1)}, pred[18]{0:T(512)(128)(4,1)}, u32[]{:S(2)}) copy-start(pred[18]{0:T(512)(128)(4,1)} %get-tuple-element.95) | copy-start | bytes 58
  760.3 17.9 %copy-start.34 = (pred[18]{0:T(512)(128)(4,1)S(1)}, pred[18]{0:T(512)(128)(4,1)}, u32[]{:S(2)}) copy-start(pred[18]{0:T(512)(128)(4,1)} %get-tuple-element.128) | copy-start | bytes 58
  760.3 19.0 %copy-start.19 = (f32[18,1,16,128]{3,0,2,1:T(8,128)S(1)}, f32[18,1,16,128]{3,0,2,1:T(8,128)}, u32[]{:S(2)}) copy-start(f32[18,1,16,128]{3,0,2,1:T(8,128)} %slice.267) | copy-start | bytes 442372
  786.5 2.6 copy-start.28
  789.1 3.8 copy-start.2
  806.2 3.0 copy-start.29
  806.2 3.0 copy-start.30
  813.9 6.6 copy-start.42
  813.9 6.7 copy-start.8
  813.9 6.7 copy-start.13
  813.9 105.3 %all-to-all-start.2 = ((bf16[32,16,16,256]{3,2,1,0:T(8,128)(2,1)}), bf16[32,16,16,256]{3,2,1,0:T(8,128)(2,1)}, u32[]{:S(2)}, u32[]{:S(2)}) async-start(bf16[32,16,16,256]{3,2,1,0:T(8,128)(2,1)} %select_select_fusion.2), calls=%async_computation.2 | async-start | bytes 8388608 | tf_op jit(solution)/shard_map/all_to_all | solution.py:153
  820.5 1.2 copy-start.21
  820.5 291.8 %all-reduce.3.cloned.1.call-start = ((), (), s32[]{:S(2)}) async-start(), calls=%async_computation.5 | async-start | bytes 3014656 | tf_op jit(solution)/shard_map/psum | solution.py:157
  821.7 1.9 copy-start.6
  821.7 1.9 copy-start.23
  823.6 1.9 copy-start.4
  827.1 97.1 %copy-start.33 = (pred[32]{0:T(512)(128)(4,1)S(1)}, pred[32]{0:T(512)(128)(4,1)}, u32[]{:S(2)}) copy-start(pred[32]{0:T(512)(128)(4,1)} %get-tuple-element.61) | copy-start | bytes 100
  924.3 195.1 %copy-start.1 = (bf16[1,32,8,8,512]{4,3,2,1,0:T(8,128)(2,1)S(1)}, bf16[1,32,8,8,512]{4,3,2,1,0:T(8,128)(2,1)}, u32[]{:S(2)}) copy-start(bf16[1,32,8,8,512]{4,3,2,1,0:T(8,128)(2,1)} %param.21) | copy-start | bytes 6291460
  (1 other events, 0.7 us)
Sparse Core Ops, SparseCore 0:
  141.4 93.4 all-gather.2
  680.2 72.1 all-gather.4
  827.8 284.4 all-reduce.2
where the time goes:
time: 1140 us; the launch traced here: 1130 us
  waiting for transfers between devices  487 us (43%)
  local copies, waits for them, and re-layouts  465 us (41%)
  other arithmetic  117 us (10%)
  starting transfers between devices  25.1 us (2%)
  matrix products  16.4 us (1%)
  between operations  15 us (1%)
    slice x9, local copies, waits for them, and re-layouts, body(): extended[:, row_tap:row_tap + span:2, col_tap:col_tap + span:2]  306 us
    psum x1, waiting for transfers between devices, body(): lax.psum((grad_reduce, grad_spatial, grad_expand, grad_shortcut), ('slide...  183 us
    all_to_all x1, waiting for transfers between devices, body(): lax.all_to_all(select_rows(blocks, send_source), 'tile', split_axis=0, co...  94.6 us
    all_to_all x1, waiting for transfers between devices, body(): lax.all_to_all(select_rows(grad_input, back_source), 'tile', split_axis=0...  92.1 us
    slice x1, local copies, waits for them, and re-layouts, body(): skip_in = work_in[:, ::2, ::2]  64.7 us
    all_gather x1, waiting for transfers between devices, body(): lax.all_gather(outgoing.astype(jnp.bfloat16), 'tile', axis=0, tiled=True)  60.1 us
    all_to_all x1, waiting for transfers between devices, body(): lax.all_to_all(select_rows(output_grad[0], send_source), 'tile', split_ax...  57.1 us
    scatter-add x9, other arithmetic, body(): grad_ext = grad_ext.at[:, row_tap:row_tap + span:2, col_tap:col_tap + spa...  55.9 us
  transfers between devices with their start and end apart: 6, of which 5 were waited for; matrix products, arithmetic and copies ran while one was open for 25% of the time, Pallas kernels for 0%

commit v1 on v0

v1 whole, which is shorter than its diff:
```python
import jax
import jax.numpy as jnp
from jax import lax
from jax.experimental import pallas as pl
from jax.experimental.pallas import tpu as pltpu
from jax.sharding import PartitionSpec as P

MESH = pl.DeviceIdType.MESH
F32 = jnp.float32
BF16 = jnp.bfloat16

ROWS = 16
OUT_ROWS = 8
WIDE = 512
HALF_WIDE = 256
MID = 128
N_XY = 16
N_Z = 8
CHUNK = 96
HALF_ROWS = N_XY * CHUNK


def nn(a, b):
    return lax.dot_general(a, b, (((1,), (0,)), ((), ())), preferred_element_type=F32)


def nt(a, b):
    return lax.dot_general(a, b, (((1,), (1,)), ((), ())), preferred_element_type=F32)


def tn(a, b):
    return lax.dot_general(a, b, (((0,), (0,)), ((), ())), preferred_element_type=F32)


def sigmoid(v):
    return 0.5 * jnp.tanh(0.5 * v) + 0.5


def kernel(
    x_hbm, bal_hbm, og_hbm, wr_hbm, wsp_hbm, we_hbm, wsc_hbm,
    ig_hbm, gr_out, gsp_out, gexp_out, gsc_out,
    xin, og, wr, wsp, we, wsc, bal,
    mask_in, mask_out, hid, dpre, even, odd, skip_f, skip, gated, gt, ga2, ga_f, wb,
    spread, gp, zskip, out_v, acc, core_in, xy_out, xy_in, z_in, done,
    x_sem, og_sem, w_sem, out_sem, halo_send, halo_recv,
    c_send, c_recv, xy_send, xy_recv, z_send, z_recv, b_send, b_recv, f_send, f_recv,
):
    s = lax.axis_index("slide")
    t = lax.axis_index("tile")
    y_lo = t // 16
    zi = (t // 2) % N_Z
    core = t % 2
    me = s * 2 + y_lo

    def xy_peer(q):
        return (q // 2, (q % 2) * 16 + t % 16)

    def z_peer(q):
        return (s, y_lo * 16 + q * 2 + core)

    core_peer = (s, t + 1 - 2 * core)
    down = (s, (t + 1) % 32)
    up = (s, (t + 31) % 32)

    def x_copy(y):
        return pltpu.make_async_copy(x_hbm.at[:, y], xin.at[y], x_sem.at[y])

    def og_copy(i):
        return pltpu.make_async_copy(og_hbm.at[:, i], og.at[i], og_sem.at[i])

    def out_copy(y):
        return pltpu.make_async_copy(out_v.at[y], ig_hbm.at[:, y], out_sem.at[y])

    w_copies = [
        pltpu.make_async_copy(a, b, w_sem.at[k])
        for k, (a, b) in enumerate(
            [(bal_hbm, bal), (wr_hbm, wr), (wsp_hbm, wsp), (we_hbm, we), (wsc_hbm, wsc)]
        )
    ]
    w_copies[0].start()
    w_copies[1].start()
    x_copy(14).start()
    x_copy(15).start()

    def start_x(y, c):
        x_copy(y).start()
        return c

    lax.fori_loop(0, ROWS - 2, start_x, 0)
    for copy in w_copies[2:]:
        copy.start()

    def start_og(i, c):
        og_copy(i).start()
        return c

    lax.fori_loop(0, OUT_ROWS, start_og, 0)

    barrier = pltpu.get_barrier_semaphore()

    def greet_xy(k, c):
        pl.semaphore_signal(barrier, 1, device_id=xy_peer((me + k) % N_XY), device_id_type=MESH)
        return c

    def greet_z(k, c):
        pl.semaphore_signal(barrier, 1, device_id=z_peer((zi + k) % N_Z), device_id_type=MESH)
        return c

    lax.fori_loop(1, N_XY, greet_xy, 0)
    lax.fori_loop(1, N_Z, greet_z, 0)
    for peer in (core_peer, down, up):
        pl.semaphore_signal(barrier, 1, device_id=peer, device_id_type=MESH)

    w_copies[0].wait()
    window = bal[:, pl.ds(pl.multiple_of((t // 4) * 128, 128), 128)]
    kept = jnp.broadcast_to(jnp.where(window >= 0, 1.0, 0.0).astype(F32), (128, 128)).astype(BF16)
    for ref, side in ((mask_in, 16), (mask_out, 8)):
        shape = ref.shape
        pixel = lax.broadcasted_iota(jnp.int32, shape, 0) // side
        lane = lax.broadcasted_iota(jnp.int32, shape, 1)
        chosen = jnp.where(lane == (t % 4) * 32 + pixel, 1.0, 0.0).astype(BF16)
        ref[...] = nt(chosen, kept)
    for slot in range(2):
        hid[slot, 0:8] = jnp.zeros((8, MID), F32)
    ga_f[HALF_WIDE : HALF_WIDE + 8] = jnp.zeros((8, MID), F32)
    acc[2944:3072] = jnp.zeros((128, 128), F32)
    zskip[...] = jnp.zeros(zskip.shape, F32)
    w_copies[1].wait()

    halo_down = pltpu.make_async_remote_copy(
        odd.at[8], odd.at[0], halo_send.at[0], halo_recv.at[0], device_id=down, device_id_type=MESH
    )
    halo_up = pltpu.make_async_remote_copy(
        ga2.at[0], ga2.at[8], halo_send.at[1], halo_recv.at[1], device_id=up, device_id_type=MESH
    )

    def hidden_pair(k, c):
        i = (k + 7) % 8
        for p in range(2):
            y = 2 * i + p
            x_copy(y).wait()
            pre = nn(xin[y].reshape(WIDE, 256), wr[...])
            sig = sigmoid(pre)
            h = pre * sig
            m = mask_in[...]
            dpre[y] = (sig + h * (1.0 - sig)) * m
            hid[p, 8 : 8 + WIDE] = h * m
            target = odd.at[i + 1] if p else even.at[i]
            for v in range(3):
                target[:, v * MID : (v + 1) * MID] = hid[p, pl.ds(7 + v, HALF_WIDE, stride=2)].astype(BF16)

        @pl.when(k == 0)
        def _():
            pl.semaphore_wait(barrier, N_XY - 1 + N_Z - 1 + 3)
            halo_down.start()

        return c

    lax.fori_loop(0, 8, hidden_pair, 0)

    for copy in w_copies[2:]:
        copy.wait()
    for u in range(3):
        tap = u * 3 * MID
        wb[u, 0:MID, 0:MID] = wsp[tap + MID : tap + 2 * MID]
        wb[u, 0:MID, MID:] = jnp.zeros((MID, MID), BF16)
        wb[u, MID:, 0:MID] = wsp[tap + 2 * MID : tap + 3 * MID]
        wb[u, MID:, MID:] = wsp[tap : tap + MID]

    def output_row(k, c):
        i = (k + 1) % 8

        @pl.when(k == 7)
        def _():
            halo_down.wait_recv()

            @pl.when(t == 0)
            def _():
                odd[0] = jnp.zeros(odd.shape[1:], BF16)

        act = nn(odd[i], wsp[0:384]) + nn(even[i], wsp[384:768]) + nn(odd[i + 1], wsp[768:1152])
        sig = sigmoid(act)
        h = act * sig
        dact = sig + h * (1.0 - sig)
        g = h.astype(BF16)
        gated[i] = g
        row = xin[2 * i].reshape(WIDE, 256).astype(F32)
        for half in range(2):
            skip_f[half] = row[:, half * 128 : (half + 1) * 128]
        for half in range(2):
            skip[i, :, half * 128 : (half + 1) * 128] = skip_f[half, pl.ds(0, HALF_WIDE, stride=2)].astype(BF16)
        total = nn(g, we[...]) + nn(skip[i], wsc[...])
        sig = sigmoid(total)
        slope = sig + total * sig * (1.0 - sig)
        og_copy(i).wait()
        m = mask_out[...]
        m = jnp.concatenate([m, m, m, m], axis=1)
        grad = og[i].astype(F32).reshape(HALF_WIDE, 512) * slope * m
        grad = grad.astype(BF16)
        gt[i] = grad
        ga = nt(grad, we[...]) * dact
        ga2[i, :, 0:MID] = ga.astype(BF16)
        ga_f[0:HALF_WIDE] = ga
        ga2[i, :, MID:] = ga_f[1 : 1 + HALF_WIDE].astype(BF16)
        return c

    lax.fori_loop(0, 8, output_row, 0)
    halo_up.start()

    gt_all = gt[...].reshape(8 * HALF_WIDE, 512)
    part = tn(skip[...].reshape(8 * HALF_WIDE, 256), gt_all)
    for k in range(4):
        acc[k * 256 : (k + 1) * 256] = part[:, k * 128 : (k + 1) * 128]
    part = tn(gated[...].reshape(8 * HALF_WIDE, MID), gt_all)
    for k in range(4):
        acc[1024 + k * 128 : 1152 + k * 128] = part[:, k * 128 : (k + 1) * 128]
    ga_all = ga2[0:8, :, 0:MID].reshape(8 * HALF_WIDE, MID)
    for u in range(3):
        taps = (odd[0:8], even[...], odd[1:9])[u].reshape(8 * HALF_WIDE, 384)
        part = tn(ga_all, taps)
        for v in range(3):
            at = 1536 + (u * 3 + v) * 128
            acc[at : at + 128] = part[:, v * 128 : (v + 1) * 128]

    def grad_pair(i, total):
        @pl.when(i == 7)
        def _():
            halo_up.wait_recv()

            @pl.when(t == 31)
            def _():
                ga2[8] = jnp.zeros(ga2.shape[1:], BF16)

        this = ga2[i]
        for p in range(2):
            y = 2 * i + p
            if p == 0:
                both = nt(this, wb[1])
            else:
                both = nt(this, wb[2]) + nt(ga2[i + 1], wb[0])
            spread[p, pl.ds(0, HALF_WIDE, stride=2)] = both[:, 0:MID]
            spread[p, pl.ds(1, HALF_WIDE, stride=2)] = both[:, MID:]
            g = (spread[p] * dpre[y]).astype(BF16)
            gp[y] = g
            total = total + tn(g, xin[y].reshape(WIDE, 256))
        return total

    part = lax.fori_loop(0, 8, grad_pair, jnp.zeros((MID, 256), F32))
    acc[2688:2816] = part[:, 0:128]
    acc[2816:2944] = part[:, 128:256]

    c_copies = []
    for k in range(4):
        rows = HALF_ROWS // 4
        c_copies.append(
            pltpu.make_async_remote_copy(
                acc.at[pl.ds(pl.multiple_of((1 - core) * HALF_ROWS + k * rows, 8), rows)],
                core_in.at[pl.ds(k * rows, rows)],
                c_send.at[k], c_recv.at[k], device_id=core_peer, device_id_type=MESH,
            )
        )
    for copy in c_copies:
        copy.start()

    def out_pair(i, c):
        back = nt(gt[i], wsc[...])
        for half in range(2):
            zskip[half, pl.ds(0, HALF_WIDE, stride=2)] = back[:, half * 128 : (half + 1) * 128]
        first = nt(gp[2 * i], wr[...]) + jnp.concatenate([zskip[0], zskip[1]], axis=1)
        out_v[2 * i] = first.astype(BF16).reshape(32, 16, 256)
        out_copy(2 * i).start()
        second = nt(gp[2 * i + 1], wr[...])
        out_v[2 * i + 1] = second.astype(BF16).reshape(32, 16, 256)
        out_copy(2 * i + 1).start()
        return c

    lax.fori_loop(0, 4, out_pair, 0)

    for copy in c_copies:
        copy.wait_recv()

    def xy_copy(q, slot):
        return pltpu.make_async_remote_copy(
            xy_out.at[q], xy_in.at[slot], xy_send.at[q], xy_recv.at[slot],
            device_id=xy_peer(q), device_id_type=MESH,
        )

    def both_cores(q):
        at = pl.multiple_of(q * CHUNK, 8)
        return acc[pl.ds(pl.multiple_of(core * HALF_ROWS + at, 8), CHUNK)] + core_in[pl.ds(at, CHUNK)]

    def send_xy(k, c):
        q = (me + k) % N_XY
        xy_out[q] = both_cores(q).astype(BF16)
        xy_copy(q, me).start()
        return c

    lax.fori_loop(1, N_XY, send_xy, 0)
    lax.fori_loop(4, 8, out_pair, 0)

    def take_xy(k, total):
        q = (me + k) % N_XY
        xy_copy(q, q).wait_recv()
        return total + xy_in[q].astype(F32)

    plane = lax.fori_loop(1, N_XY, take_xy, both_cores(me))

    z_in[zi] = plane.astype(BF16)

    def z_copy(q, slot):
        return pltpu.make_async_remote_copy(
            z_in.at[zi], z_in.at[slot], z_send.at[q], z_recv.at[slot],
            device_id=z_peer(q), device_id_type=MESH,
        )

    def send_z(k, c):
        z_copy((zi + k) % N_Z, zi).start()
        return c

    lax.fori_loop(1, N_Z, send_z, 0)

    def take_z(k, c):
        q = (zi + k) % N_Z
        z_copy(q, q).wait_recv()
        return c

    lax.fori_loop(1, N_Z, take_z, 0)
    whole = z_in[0].astype(F32)
    for q in range(1, N_Z):
        whole = whole + z_in[q].astype(F32)

    mine = core * N_XY
    done[mine + me] = whole.astype(BF16)

    def back_copy(q, slot):
        return pltpu.make_async_remote_copy(
            done.at[mine + me], done.at[mine + slot], b_send.at[q], b_recv.at[slot],
            device_id=xy_peer(q), device_id_type=MESH,
        )

    def pass_copy(q, side):
        return pltpu.make_async_remote_copy(
            done.at[mine + q], done.at[side * N_XY + q], f_send.at[q], f_recv.at[q],
            device_id=core_peer, device_id_type=MESH,
        )

    def send_back(k, c):
        back_copy((me + k) % N_XY, me).start()
        return c

    lax.fori_loop(1, N_XY, send_back, 0)
    pass_copy(me, core).start()

    def pass_on(k, c):
        q = (me + k) % N_XY
        back_copy(q, q).wait_recv()
        pass_copy(q, core).start()
        return c

    lax.fori_loop(1, N_XY, pass_on, 0)

    def take_passed(q, c):
        pass_copy(q, 1 - core).wait_recv()
        return c

    lax.fori_loop(0, N_XY, take_passed, 0)

    packed = done[...].astype(F32).reshape(2 * HALF_ROWS, 128)
    for k in range(4):
        gsc_out[:, k * 128 : (k + 1) * 128] = packed[k * 256 : (k + 1) * 256]
        gexp_out[:, k * 128 : (k + 1) * 128] = packed[1024 + k * 128 : 1152 + k * 128]
    for k in range(9):
        gsp_out[k * 128 : (k + 1) * 128] = packed[1536 + k * 128 : 1664 + k * 128].T
    for k in range(2):
        gr_out[k * 128 : (k + 1) * 128] = packed[2688 + k * 128 : 2816 + k * 128].T

    halo_down.wait_send()
    halo_up.wait_send()
    for copy in c_copies:
        copy.wait_send()

    def sent_xy(k, c):
        q = (me + k) % N_XY
        xy_copy(q, me).wait_send()
        back_copy(q, me).wait_send()
        return c

    lax.fori_loop(1, N_XY, sent_xy, 0)

    def sent_z(k, c):
        z_copy((zi + k) % N_Z, zi).wait_send()
        return c

    lax.fori_loop(1, N_Z, sent_z, 0)

    def sent_pass(q, c):
        pass_copy(q, core).wait_send()
        return c

    lax.fori_loop(0, N_XY, sent_pass, 0)

    def written(y, c):
        out_copy(y).wait()
        return c

    lax.fori_loop(0, ROWS, written, 0)


def body(slide_tiles, balance_list, output_grad, w_reduce, w_spatial, w_expand, w_shortcut):
    dma = pltpu.SemaphoreType.DMA
    any_spec = pl.BlockSpec(memory_space=pl.ANY)
    vmem_spec = pl.BlockSpec(memory_space=pltpu.VMEM)
    out = pl.pallas_call(
        kernel,
        out_shape=(
            jax.ShapeDtypeStruct((32, 16, 16, 256), BF16),
            jax.ShapeDtypeStruct((256, 128), F32),
            jax.ShapeDtypeStruct((1152, 128), F32),
            jax.ShapeDtypeStruct((128, 512), F32),
            jax.ShapeDtypeStruct((256, 512), F32),
        ),
        in_specs=[any_spec] * 7,
        out_specs=(any_spec, vmem_spec, vmem_spec, vmem_spec, vmem_spec),
        scratch_shapes=[
            pltpu.VMEM((16, 32, 16, 256), BF16),
            pltpu.VMEM((8, 32, 8, 512), BF16),
            pltpu.VMEM((256, 128), BF16),
            pltpu.VMEM((1152, 128), BF16),
            pltpu.VMEM((128, 512), BF16),
            pltpu.VMEM((256, 512), BF16),
            pltpu.VMEM((1, 1024), jnp.int32),
            pltpu.VMEM((WIDE, 128), F32),
            pltpu.VMEM((HALF_WIDE, 128), F32),
            pltpu.VMEM((2, WIDE + 16, MID), F32),
            pltpu.VMEM((16, WIDE, MID), F32),
            pltpu.VMEM((8, HALF_WIDE, 384), BF16),
            pltpu.VMEM((9, HALF_WIDE, 384), BF16),
            pltpu.VMEM((2, WIDE, 128), F32),
            pltpu.VMEM((8, HALF_WIDE, 256), BF16),
            pltpu.VMEM((8, HALF_WIDE, MID), BF16),
            pltpu.VMEM((8, HALF_WIDE, 512), BF16),
            pltpu.VMEM((9, HALF_WIDE, 256), BF16),
            pltpu.VMEM((HALF_WIDE + 8, MID), F32),
            pltpu.VMEM((3, 256, 256), BF16),
            pltpu.VMEM((2, WIDE, MID), F32),
            pltpu.VMEM((16, WIDE, MID), BF16),
            pltpu.VMEM((2, WIDE, 128), F32),
            pltpu.VMEM((16, 32, 16, 256), BF16),
            pltpu.VMEM((2 * HALF_ROWS, 128), F32),
            pltpu.VMEM((HALF_ROWS, 128), F32),
            pltpu.VMEM((N_XY, CHUNK, 128), BF16),
            pltpu.VMEM((N_XY, CHUNK, 128), BF16),
            pltpu.VMEM((N_Z, CHUNK, 128), BF16),
            pltpu.VMEM((2 * N_XY, CHUNK, 128), BF16),
            dma((16,)),
            dma((8,)),
            dma((5,)),
            dma((16,)),
            dma((2,)),
            dma((2,)),
            dma((4,)),
            dma((4,)),
            dma((N_XY,)),
            dma((N_XY,)),
            dma((N_Z,)),
            dma((N_Z,)),
            dma((N_XY,)),
            dma((N_XY,)),
            dma((N_XY,)),
            dma((N_XY,)),
        ],
        compiler_params=pltpu.CompilerParams(
            collective_id=0, has_side_effects=True, vmem_limit_bytes=56 * 2**20
        ),
    )(slide_tiles[0], balance_list, output_grad[0], w_reduce, w_spatial, w_expand, w_shortcut)
    return (out[0][None], out[1], out[2], out[3], out[4])


def solution(mesh):
    in_specs = (
        P("slide", "tile", None, None, None),
        P("slide", None),
        P("slide", "tile", None, None, None),
        P(),
        P(),
        P(),
        P(),
    )
    out_specs = (P("slide", "tile", None, None, None), P(), P(), P(), P())
    return jax.shard_map(body, mesh=mesh, in_specs=in_specs, out_specs=out_specs, check_vma=False)
```

time: 1140 us -> 69.3 us (0.06); the launches traced: 1130 us -> 69.2 us
  waiting for transfers between devices: 487 us -> 0 us
  local copies, waits for them, and re-layouts: 465 us -> 7.73 us
  other arithmetic: 117 us -> 0 us
  Pallas kernels: 0 us -> 60.8 us
  starting transfers between devices: 25.1 us -> 0 us
  matrix products: 16.4 us -> 0 us
  between operations: 15 us -> 0.68 us
    slice x22 -> x0, local copies, waits for them, and re-layouts: 383 us -> none  [the longest x9 306 us: body(): extended[:, row_tap:row_tap + span:2, col_tap:col_tap + span:2]]
    all_to_all x3 -> x0, waiting for transfers between devices: 244 us -> none  [the longest x1 94.6 us: body(): lax.all_to_all(select_rows(blocks, send_source), 'tile', split_axis=0, co...]
    psum x1 -> x0, waiting for transfers between devices: 183 us -> none  [body(): lax.psum((grad_reduce, grad_spatial, grad_expand, grad_shortcut), ('slide...]
    scatter-add x11 -> x0, other arithmetic: 65.1 us -> none  [the longest x9 55.9 us: body(): grad_ext = grad_ext.at[:, row_tap:row_tap + span:2, col_tap:col_tap + spa...]
    pallas_call x0 -> x1, Pallas kernels: none -> 60.8 us  [body(): pl.pallas_call(kernel, out_shape=(jax.ShapeDtypeStruct((32, 16, 16, 256),...]
    all_gather x2 -> x0, waiting for transfers between devices: 60.1 us -> none  [the longest x1 60.1 us: body(): lax.all_gather(outgoing.astype(jnp.bfloat16), 'tile', axis=0, tiled=True)]
    gather x12 -> x0, local copies, waits for them, and re-layouts: 46.6 us -> none  [select_rows(): taken = jnp.take(table, safe, axis=0)]
    all_to_all x3 -> x0, starting transfers between devices: 25 us -> none  [the longest x1 11.2 us: body(): lax.all_to_all(select_rows(blocks, send_source), 'tile', split_axis=0, co...]
  transfers between devices with their start and end apart: 6 -> 0, of which waited for: 5 -> 0; matrix products, arithmetic and copies ran while one was open for 25% -> 0% of each run, Pallas kernels for 0% -> 0%
where the time goes in v1:
time: 69.3 us; the launch traced here: 69.2 us
  Pallas kernels  60.8 us (88%)
  local copies, waits for them, and re-layouts  7.73 us (11%)
    pallas_call x1, Pallas kernels, body(): pl.pallas_call(kernel, out_shape=(jax.ShapeDtypeStruct((32, 16, 16, 256),...  60.8 us
    unnamed x13, local copies, waits for them, and re-layouts  7.73 us

profile of v1, /device:TPU:1, one launch (start us, length us, event | category | flops | bytes accessed | tf_op | source)
XLA Modules:
  0.0 69.2 jit_solution(12822804140030816198)
XLA Ops:
  0.6 60.8 %shard_map.110 = (bf16[32,16,16,256]{3,2,1,0:T(8,128)(2,1)}, f32[256,128]{1,0:T(8,128)}, f32[1152,128]{1,0:T(8,128)}, f32[128,512]{1,0:T(8,128)}, f32[256,512]{1,0:T(8,128)}) custom-call(bf16[32,16,16,256]{3,2,1,0:T(8,128)(2,1)} %bitcast.3, s32[1,1024]{1,0:T(1,128)} %bal_hbm.1, bf16[32,8,8,512]{3,2,1,0:T(8,128)(2,1)} %bitcast.5, bf16[256,128]{1,0:T(8,128)(2,1)} %wr_hbm.1, ...), custom_call_target="tpu_custom_call" | custom-call | tf_op jit(solution)/shard_map/pallas_call | solution.py:413
  61.4 0.0 copy-start.3
  61.4 0.0 copy-start
  61.5 0.0 copy-start.2
  61.5 0.0 copy-start.1
  61.5 4.8 %copy.17 = bf16[1,32,16,16,256]{4,3,2,1,0:T(8,128)(2,1)} copy(bf16[1,32,16,16,256]{4,3,2,1,0:T(8,128)(2,1)} %bitcast.4) | data formatting | bytes 8388608
  66.2 0.0 copy-done.3
  66.2 0.7 copy.18
  66.9 0.0 copy-done
  66.9 0.8 %copy.19 = f32[1152,128]{1,0:T(8,128)} copy(f32[1152,128]{1,0:T(8,128)S(1)} %copy-done) | data formatting | bytes 1179648
  67.7 0.0 copy-done.2
  67.7 0.7 %copy.20 = f32[128,512]{1,0:T(8,128)} copy(f32[128,512]{1,0:T(8,128)S(1)} %copy-done.2) | data formatting | bytes 524288
  68.4 0.0 copy-done.1
  68.4 0.8 %copy.21 = f32[256,512]{1,0:T(8,128)} copy(f32[256,512]{1,0:T(8,128)S(1)} %copy-done.1) | data formatting | bytes 1048576
Async XLA Ops:
  61.4 4.8 %copy-start.3 = (f32[256,128]{1,0:T(8,128)S(1)}, f32[256,128]{1,0:T(8,128)}, u32[]{:S(2)}) copy-start(f32[256,128]{1,0:T(8,128)} %get-tuple-element.21) | copy-start | bytes 393220
  61.4 5.4 %copy-start = (f32[1152,128]{1,0:T(8,128)S(1)}, f32[1152,128]{1,0:T(8,128)}, u32[]{:S(2)}) copy-start(f32[1152,128]{1,0:T(8,128)} %get-tuple-element.22) | copy-start | bytes 1769476
  61.5 6.2 %copy-start.2 = (f32[128,512]{1,0:T(8,128)S(1)}, f32[128,512]{1,0:T(8,128)}, u32[]{:S(2)}) copy-start(f32[128,512]{1,0:T(8,128)} %get-tuple-element.23) | copy-start | bytes 786436
  61.5 6.9 %copy-start.1 = (f32[256,512]{1,0:T(8,128)S(1)}, f32[256,512]{1,0:T(8,128)}, u32[]{:S(2)}) copy-start(f32[256,512]{1,0:T(8,128)} %get-tuple-element.24) | copy-start | bytes 1572868

commit v2 on v1

v2 whole, which is shorter than its diff:
```python
import jax
import jax.numpy as jnp
from jax import lax
from jax.experimental import pallas as pl
from jax.experimental.pallas import tpu as pltpu
from jax.sharding import PartitionSpec as P

MESH = pl.DeviceIdType.MESH
F32 = jnp.float32
BF16 = jnp.bfloat16

ROWS = 16
OUT_ROWS = 8
WIDE = 512
HALF_WIDE = 256
MID = 128
N_XY = 16
N_Z = 8
CHUNKS = (80, 16)
CHUNK = 96
SHARE = 12


def nn(a, b):
    return lax.dot_general(a, b, (((1,), (0,)), ((), ())), preferred_element_type=F32)


def nt(a, b):
    return lax.dot_general(a, b, (((1,), (1,)), ((), ())), preferred_element_type=F32)


def tn(a, b):
    return lax.dot_general(a, b, (((0,), (0,)), ((), ())), preferred_element_type=F32)


def silu_parts(half, scale=None):
    u = jnp.tanh(half)
    twice = 1.0 + u
    if scale is not None:
        twice = twice * scale
    h = half * twice
    return h, twice + h * (1.0 - u)


def kernel(
    x_hbm, bal_hbm, og_hbm, wr_hbm, wsp_hbm, we_hbm, wsc_hbm,
    out_v, done,
    xin, og, wr, wsp, we, wsc, bal,
    mask_in, mask_out, hid, dpre, even, odd, skip_f, skip, gated, gt, ga2, ga_f, wb,
    spread, gp, zskip, wr_h, wsp_h, we_h, wsc_h,
    acc_a, acc_b, core_a, core_b, xy_out_a, xy_out_b, xy_in_a, xy_in_b, plane_f, z_out, z_in, z_done,
    x_sem, og_sem, w_sem, halo_send, halo_recv,
    c_send, c_recv, xy_send_a, xy_send_b, xy_recv_a, xy_recv_b, z_send, z_recv, g_send, g_recv,
    b_send, b_recv, f_send, f_recv,
):
    s = lax.axis_index("slide")
    t = lax.axis_index("tile")
    y_lo = t // 16
    zi = (t // 2) % N_Z
    core = t % 2
    me = s * 2 + y_lo

    def xy_peer(q):
        return (q // 2, (q % 2) * 16 + t % 16)

    def z_peer(q):
        return (s, y_lo * 16 + q * 2 + core)

    core_peer = (s, t + 1 - 2 * core)
    down = (s, (t + 1) % 32)
    up = (s, (t + 31) % 32)

    def x_copy(y):
        return pltpu.make_async_copy(x_hbm.at[:, y], xin.at[y], x_sem.at[y])

    def og_copy(i):
        return pltpu.make_async_copy(og_hbm.at[:, i], og.at[i], og_sem.at[i])

    w_copies = [
        pltpu.make_async_copy(a, b, w_sem.at[k])
        for k, (a, b) in enumerate(
            [(bal_hbm, bal), (wr_hbm, wr), (wsp_hbm, wsp), (we_hbm, we), (wsc_hbm, wsc)]
        )
    ]
    w_copies[0].start()
    w_copies[1].start()
    x_copy(14).start()
    x_copy(15).start()

    def start_x(y, c):
        x_copy(y).start()
        return c

    lax.fori_loop(0, ROWS - 2, start_x, 0)
    for copy in w_copies[2:]:
        copy.start()

    def start_og(i, c):
        og_copy(i).start()
        return c

    lax.fori_loop(0, OUT_ROWS, start_og, 0)

    barrier = pltpu.get_barrier_semaphore()

    def greet_xy(k, c):
        pl.semaphore_signal(barrier, 1, device_id=xy_peer((me + k) % N_XY), device_id_type=MESH)
        return c

    def greet_z(k, c):
        pl.semaphore_signal(barrier, 1, device_id=z_peer((zi + k) % N_Z), device_id_type=MESH)
        return c

    lax.fori_loop(1, N_XY, greet_xy, 0)
    lax.fori_loop(1, N_Z, greet_z, 0)
    for peer in (core_peer, down, up):
        pl.semaphore_signal(barrier, 1, device_id=peer, device_id_type=MESH)

    w_copies[0].wait()
    window = bal[:, pl.ds(pl.multiple_of((t // 4) * 128, 128), 128)]
    kept = jnp.broadcast_to(jnp.where(window >= 0, 1.0, 0.0).astype(F32), (128, 128)).astype(BF16)
    for ref, side, scale in ((mask_in, 16, 1.0), (mask_out, 8, 0.5)):
        shape = ref.shape
        pixel = lax.broadcasted_iota(jnp.int32, shape, 0) // side
        lane = lax.broadcasted_iota(jnp.int32, shape, 1)
        chosen = jnp.where(lane == (t % 4) * 32 + pixel, 1.0, 0.0).astype(BF16)
        ref[...] = nt(chosen, kept) * scale
    for slot in range(2):
        hid[slot, 0:8] = jnp.zeros((8, MID), F32)
    ga_f[HALF_WIDE : HALF_WIDE + 8] = jnp.zeros((8, MID), F32)
    acc_b[384:512] = jnp.zeros((128, 128), F32)
    zskip[...] = jnp.zeros(zskip.shape, F32)
    w_copies[1].wait()
    wr_h[...] = wr[...] * jnp.asarray(0.5, BF16)

    halo_down = pltpu.make_async_remote_copy(
        odd.at[8], odd.at[0], halo_send.at[0], halo_recv.at[0], device_id=down, device_id_type=MESH
    )
    halo_up = pltpu.make_async_remote_copy(
        ga2.at[0], ga2.at[8], halo_send.at[1], halo_recv.at[1], device_id=up, device_id_type=MESH
    )

    def hidden_pair(k, c):
        i = (k + 7) % 8
        for p in range(2):
            y = 2 * i + p
            x_copy(y).wait()
            h, slope = silu_parts(nn(xin[y].reshape(WIDE, 256), wr_h[...]), mask_in[...])
            dpre[y] = slope
            hid[p, 8 : 8 + WIDE] = h
            target = odd.at[i + 1] if p else even.at[i]
            for v in range(3):
                target[:, v * MID : (v + 1) * MID] = hid[p, pl.ds(7 + v, HALF_WIDE, stride=2)].astype(BF16)

        return c

    lax.fori_loop(0, 8, hidden_pair, 0)
    pl.semaphore_wait(barrier, N_XY - 1 + N_Z - 1 + 3)
    halo_down.start()

    for copy in w_copies[2:]:
        copy.wait()
    for to, of in ((wsp_h, wsp), (we_h, we), (wsc_h, wsc)):
        to[...] = of[...] * jnp.asarray(0.5, BF16)
    for u in range(3):
        tap = u * 3 * MID
        wb[u, 0:MID, 0:MID] = wsp_h[tap + MID : tap + 2 * MID]
        wb[u, 0:MID, MID:] = jnp.zeros((MID, MID), BF16)
        wb[u, MID:, 0:MID] = wsp_h[tap + 2 * MID : tap + 3 * MID]
        wb[u, MID:, MID:] = wsp_h[tap : tap + MID]

    def output_row(k, c):
        i = (k + 1) % 8

        @pl.when(k == 7)
        def _():
            halo_down.wait_recv()

            @pl.when(t == 0)
            def _():
                odd[0] = jnp.zeros(odd.shape[1:], BF16)

        half = nn(odd[i], wsp_h[0:384]) + nn(even[i], wsp_h[384:768]) + nn(odd[i + 1], wsp_h[768:1152])
        h, dact = silu_parts(half)
        g = h.astype(BF16)
        gated[i] = g
        row = xin[2 * i].reshape(WIDE, 256).astype(F32)
        for half in range(2):
            skip_f[half] = row[:, half * 128 : (half + 1) * 128]
        for half in range(2):
            skip[i, :, half * 128 : (half + 1) * 128] = skip_f[half, pl.ds(0, HALF_WIDE, stride=2)].astype(BF16)
        half = nn(g, we_h[...]) + nn(skip[i], wsc_h[...])
        og_copy(i).wait()
        m = mask_out[...]
        m = jnp.concatenate([m, m, m, m], axis=1)
        _, slope = silu_parts(half, m)
        grad = (og[i].astype(F32).reshape(HALF_WIDE, 512) * slope).astype(BF16)
        gt[i] = grad
        ga = nt(grad, we_h[...]) * dact
        ga2[i, :, 0:MID] = ga.astype(BF16)
        ga_f[0:HALF_WIDE] = ga
        ga2[i, :, MID:] = ga_f[1 : 1 + HALF_WIDE].astype(BF16)
        return c

    lax.fori_loop(0, 8, output_row, 0)
    halo_up.start()

    gt_all = gt[...].reshape(8 * HALF_WIDE, 512)
    part = tn(skip[...].reshape(8 * HALF_WIDE, 256), gt_all)
    for k in range(4):
        acc_a[k * 256 : (k + 1) * 256] = part[:, k * 128 : (k + 1) * 128]
    part = tn(gated[...].reshape(8 * HALF_WIDE, MID), gt_all)
    for k in range(4):
        acc_a[1024 + k * 128 : 1152 + k * 128] = part[:, k * 128 : (k + 1) * 128]
    ga_all = ga2[0:8, :, 0:MID].reshape(8 * HALF_WIDE, MID)
    for u in range(3):
        taps = (odd[0:8], even[...], odd[1:9])[u].reshape(8 * HALF_WIDE, 384)
        part = tn(ga_all, taps)
        for v in range(3):
            tap = u * 3 + v
            to, at = (acc_a, 1536 + tap * 128) if tap < 8 else (acc_b, 0)
            to[at : at + 128] = part[:, v * 128 : (v + 1) * 128]

    def grad_pair(i, total):
        @pl.when(i == 7)
        def _():
            halo_up.wait_recv()

            @pl.when(t == 31)
            def _():
                ga2[8] = jnp.zeros(ga2.shape[1:], BF16)

        this = ga2[i]
        for p in range(2):
            y = 2 * i + p
            if p == 0:
                both = nt(this, wb[1])
            else:
                both = nt(this, wb[2]) + nt(ga2[i + 1], wb[0])
            spread[p, pl.ds(0, HALF_WIDE, stride=2)] = both[:, 0:MID]
            spread[p, pl.ds(1, HALF_WIDE, stride=2)] = both[:, MID:]
            g = (spread[p] * dpre[y]).astype(BF16)
            gp[y] = g
            total = total + tn(g, xin[y].reshape(WIDE, 256))
        return total

    def out_pair(i, c):
        back = nt(gt[i], wsc[...])
        for half in range(2):
            zskip[half, pl.ds(0, HALF_WIDE, stride=2)] = back[:, half * 128 : (half + 1) * 128]
        first = nt(gp[2 * i], wr[...]) + jnp.concatenate([zskip[0], zskip[1]], axis=1)
        out_v[2 * i] = first.astype(BF16).reshape(32, 16, 256)
        second = nt(gp[2 * i + 1], wr[...])
        out_v[2 * i + 1] = second.astype(BF16).reshape(32, 16, 256)
        return c

    accs, cores = (acc_a, acc_b), (core_a, core_b)
    xy_outs, xy_ins = (xy_out_a, xy_out_b), (xy_in_a, xy_in_b)
    xy_sends, xy_recvs = (xy_send_a, xy_send_b), (xy_recv_a, xy_recv_b)

    def core_copy(part):
        rows = N_XY * CHUNKS[part]
        return pltpu.make_async_remote_copy(
            accs[part].at[pl.ds(pl.multiple_of((1 - core) * rows, 8), rows)], cores[part],
            c_send.at[part], c_recv.at[part], device_id=core_peer, device_id_type=MESH,
        )

    def xy_copy(part, q, slot):
        return pltpu.make_async_remote_copy(
            xy_outs[part].at[q], xy_ins[part].at[slot], xy_sends[part].at[q], xy_recvs[part].at[slot],
            device_id=xy_peer(q), device_id_type=MESH,
        )

    def both_cores(part, q):
        chunk = CHUNKS[part]
        at = pl.multiple_of(q * chunk, 8)
        kept = accs[part][pl.ds(pl.multiple_of(core * (N_XY * chunk) + at, 8), chunk)]
        return kept + cores[part][pl.ds(at, chunk)]

    def send_xy(part):
        def step(k, c):
            q = (me + k) % N_XY
            xy_outs[part][q] = both_cores(part, q).astype(BF16)
            xy_copy(part, q, me).start()
            return c

        lax.fori_loop(1, N_XY, step, 0)

    def take_xy(part):
        def step(k, total):
            q = (me + N_XY - k) % N_XY
            xy_copy(part, q, q).wait_recv()
            return total + xy_ins[part][q].astype(F32)

        return lax.fori_loop(1, N_XY, step, both_cores(part, me))

    def z_copy(q, slot):
        return pltpu.make_async_remote_copy(
            z_out.at[q], z_in.at[slot], z_send.at[q], z_recv.at[slot],
            device_id=z_peer(q), device_id_type=MESH,
        )

    def share_copy(q, slot):
        return pltpu.make_async_remote_copy(
            z_done.at[zi], z_done.at[slot], g_send.at[q], g_recv.at[slot],
            device_id=z_peer(q), device_id_type=MESH,
        )

    def send_z(k, c):
        z_copy((zi + k) % N_Z, zi).start()
        return c

    def take_z(k, c):
        q = (zi + N_Z - k) % N_Z
        z_copy(q, q).wait_recv()
        return c

    def send_share(k, c):
        share_copy((zi + k) % N_Z, zi).start()
        return c

    def take_share(k, c):
        q = (zi + N_Z - k) % N_Z
        share_copy(q, q).wait_recv()
        return c

    mine = core * N_XY

    def back_copy(q, slot):
        return pltpu.make_async_remote_copy(
            done.at[mine + me], done.at[mine + slot], b_send.at[q], b_recv.at[slot],
            device_id=xy_peer(q), device_id_type=MESH,
        )

    def pass_copy(q, side):
        return pltpu.make_async_remote_copy(
            done.at[mine + q], done.at[side * N_XY + q], f_send.at[q], f_recv.at[q],
            device_id=core_peer, device_id_type=MESH,
        )

    def send_back(k, c):
        back_copy((me + k) % N_XY, me).start()
        return c

    def pass_on(k, c):
        q = (me + N_XY - k) % N_XY
        back_copy(q, q).wait_recv()
        pass_copy(q, core).start()
        return c

    def take_passed(k, c):
        pass_copy((me + N_XY - k) % N_XY, 1 - core).wait_recv()
        return c

    core_copy(0).start()
    total = lax.fori_loop(0, 2, grad_pair, jnp.zeros((MID, 256), F32))
    core_copy(0).wait_recv()
    send_xy(0)
    total = lax.fori_loop(2, 8, grad_pair, total)
    acc_b[128:256] = total[:, 0:128]
    acc_b[256:384] = total[:, 128:256]
    core_copy(1).start()
    lax.fori_loop(0, 3, out_pair, 0)
    core_copy(1).wait_recv()
    send_xy(1)
    lax.fori_loop(3, 6, out_pair, 0)
    plane_f[0:80] = take_xy(0)
    plane_f[80:96] = take_xy(1)
    for q in range(N_Z):
        z_out[q, 0:SHARE] = plane_f[q * SHARE : (q + 1) * SHARE].astype(BF16)
    z_in[zi] = z_out[zi]
    lax.fori_loop(1, N_Z, send_z, 0)
    lax.fori_loop(6, 7, out_pair, 0)
    lax.fori_loop(1, N_Z, take_z, 0)
    share = z_in[0, 0:SHARE].astype(F32)
    for q in range(1, N_Z):
        share = share + z_in[q, 0:SHARE].astype(F32)
    z_done[zi, 0:SHARE] = share.astype(BF16)
    lax.fori_loop(1, N_Z, send_share, 0)
    lax.fori_loop(7, 8, out_pair, 0)
    lax.fori_loop(1, N_Z, take_share, 0)
    for q in range(N_Z):
        plane_f[q * SHARE : (q + 1) * SHARE] = z_done[q, 0:SHARE].astype(F32)
    done[mine + me] = plane_f[...].astype(BF16)
    lax.fori_loop(1, N_XY, send_back, 0)
    pass_copy(me, core).start()
    lax.fori_loop(1, N_XY, pass_on, 0)
    lax.fori_loop(0, N_XY, take_passed, 0)

    halo_down.wait_send()
    halo_up.wait_send()
    for part in range(2):
        core_copy(part).wait_send()

    def sent_xy(k, c):
        q = (me + k) % N_XY
        for part in range(2):
            xy_copy(part, q, me).wait_send()
        back_copy(q, me).wait_send()
        return c

    lax.fori_loop(1, N_XY, sent_xy, 0)

    def sent_z(k, c):
        q = (zi + k) % N_Z
        z_copy(q, zi).wait_send()
        share_copy(q, zi).wait_send()
        return c

    lax.fori_loop(1, N_Z, sent_z, 0)

    def sent_pass(q, c):
        pass_copy(q, core).wait_send()
        return c

    lax.fori_loop(0, N_XY, sent_pass, 0)


def write_out(
    out_v, done, ig_hbm, gr_hbm, gsp_hbm, gexp_hbm, gsc_hbm, gr, gsp, gexp, gsc, out_sem, w_sem
):
    copies = [
        pltpu.make_async_copy(out_v.at[y], ig_hbm.at[:, y], out_sem.at[y]) for y in range(ROWS)
    ]
    for copy in copies:
        copy.start()
    part = done[:, 0:80].astype(F32).reshape(2560, 128)
    last = done[:, 80:96].astype(F32).reshape(512, 128)
    for k in range(4):
        gsc[:, k * 128 : (k + 1) * 128] = part[k * 256 : (k + 1) * 256]
        gexp[:, k * 128 : (k + 1) * 128] = part[1024 + k * 128 : 1152 + k * 128]
    for k in range(8):
        gsp[k * 128 : (k + 1) * 128] = part[1536 + k * 128 : 1664 + k * 128].T
    gsp[1024:1152] = last[0:128].T
    for k in range(2):
        gr[k * 128 : (k + 1) * 128] = last[128 + k * 128 : 256 + k * 128].T
    pairs = ((gr, gr_hbm), (gsp, gsp_hbm), (gexp, gexp_hbm), (gsc, gsc_hbm))
    more = [pltpu.make_async_copy(a, b, w_sem.at[k]) for k, (a, b) in enumerate(pairs)]
    for copy in more:
        copy.start()
    for copy in copies + more:
        copy.wait()


def body(slide_tiles, balance_list, output_grad, w_reduce, w_spatial, w_expand, w_shortcut):
    dma = pltpu.SemaphoreType.DMA
    any_spec = pl.BlockSpec(memory_space=pltpu.HBM)
    vmem_spec = pl.BlockSpec(memory_space=pltpu.VMEM)
    out_v, done = pl.pallas_call(
        kernel,
        out_shape=(
            pltpu.VMEM((16, 32, 16, 256), BF16),
            pltpu.VMEM((2 * N_XY, CHUNK, 128), BF16),
        ),
        in_specs=[any_spec] * 7,
        out_specs=(vmem_spec, vmem_spec),
        scratch_shapes=[
            pltpu.VMEM((16, 32, 16, 256), BF16),
            pltpu.VMEM((8, 32, 8, 512), BF16),
            pltpu.VMEM((256, 128), BF16),
            pltpu.VMEM((1152, 128), BF16),
            pltpu.VMEM((128, 512), BF16),
            pltpu.VMEM((256, 512), BF16),
            pltpu.VMEM((1, 1024), jnp.int32),
            pltpu.VMEM((WIDE, 128), F32),
            pltpu.VMEM((HALF_WIDE, 128), F32),
            pltpu.VMEM((2, WIDE + 16, MID), F32),
            pltpu.VMEM((16, WIDE, MID), F32),
            pltpu.VMEM((8, HALF_WIDE, 384), BF16),
            pltpu.VMEM((9, HALF_WIDE, 384), BF16),
            pltpu.VMEM((2, WIDE, 128), F32),
            pltpu.VMEM((8, HALF_WIDE, 256), BF16),
            pltpu.VMEM((8, HALF_WIDE, MID), BF16),
            pltpu.VMEM((8, HALF_WIDE, 512), BF16),
            pltpu.VMEM((9, HALF_WIDE, 256), BF16),
            pltpu.VMEM((HALF_WIDE + 8, MID), F32),
            pltpu.VMEM((3, 256, 256), BF16),
            pltpu.VMEM((2, WIDE, MID), F32),
            pltpu.VMEM((16, WIDE, MID), BF16),
            pltpu.VMEM((2, WIDE, 128), F32),
            pltpu.VMEM((256, 128), BF16),
            pltpu.VMEM((1152, 128), BF16),
            pltpu.VMEM((128, 512), BF16),
            pltpu.VMEM((256, 512), BF16),
            pltpu.VMEM((2560, 128), F32),
            pltpu.VMEM((512, 128), F32),
            pltpu.VMEM((1280, 128), F32),
            pltpu.VMEM((256, 128), F32),
            pltpu.VMEM((N_XY, 80, 128), BF16),
            pltpu.VMEM((N_XY, 16, 128), BF16),
            pltpu.VMEM((N_XY, 80, 128), BF16),
            pltpu.VMEM((N_XY, 16, 128), BF16),
            pltpu.VMEM((CHUNK, 128), F32),
            pltpu.VMEM((N_Z, 16, 128), BF16),
            pltpu.VMEM((N_Z, 16, 128), BF16),
            pltpu.VMEM((N_Z, 16, 128), BF16),
            dma((16,)),
            dma((8,)),
            dma((5,)),
            dma((2,)),
            dma((2,)),
            dma((2,)),
            dma((2,)),
            dma((N_XY,)),
            dma((N_XY,)),
            dma((N_XY,)),
            dma((N_XY,)),
            dma((N_Z,)),
            dma((N_Z,)),
            dma((N_Z,)),
            dma((N_Z,)),
            dma((N_XY,)),
            dma((N_XY,)),
            dma((N_XY,)),
            dma((N_XY,)),
        ],
        compiler_params=pltpu.CompilerParams(
            collective_id=0, has_side_effects=True, vmem_limit_bytes=59 * 2**20
        ),
    )(slide_tiles[0], balance_list, output_grad[0], w_reduce, w_spatial, w_expand, w_shortcut)
    shapes = ((256, 128), (1152, 128), (128, 512), (256, 512))
    out = pl.pallas_call(
        write_out,
        out_shape=[jax.ShapeDtypeStruct((32, 16, 16, 256), BF16)]
        + [jax.ShapeDtypeStruct(shape, F32) for shape in shapes],
        in_specs=[vmem_spec, vmem_spec],
        out_specs=[any_spec] * 5,
        scratch_shapes=[pltpu.VMEM(shape, F32) for shape in shapes] + [dma((16,)), dma((4,))],
        compiler_params=pltpu.CompilerParams(vmem_limit_bytes=16 * 2**20),
    )(out_v, done)
    return (out[0][None], out[1], out[2], out[3], out[4])


def solution(mesh):
    in_specs = (
        P("slide", "tile", None, None, None),
        P("slide", None),
        P("slide", "tile", None, None, None),
        P(),
        P(),
        P(),
        P(),
    )
    out_specs = (P("slide", "tile", None, None, None), P(), P(), P(), P())
    return jax.shard_map(body, mesh=mesh, in_specs=in_specs, out_specs=out_specs, check_vma=False)
```

time: 69.3 us -> 56.9 us (0.82)
  local copies, waits for them, and re-layouts: 7.73 us -> 0 us
  Pallas kernels: 60.8 us -> 56.2 us
    unnamed x13 -> x0, local copies, waits for them, and re-layouts: 7.73 us -> none
    pallas_call x1 -> x2, Pallas kernels: 60.8 us -> 56.2 us  [the longest x1 53.5 us: body(): pl.pallas_call(kernel, out_shape=(pltpu.VMEM((16, 32, 16, 256), BF16), pl...]
where the time goes in v2:
time: 56.9 us; the launch traced here: 56.8 us
  Pallas kernels  56.2 us (99%)
  between operations  0.64 us (1%)
    pallas_call x1, Pallas kernels, body(): pl.pallas_call(kernel, out_shape=(pltpu.VMEM((16, 32, 16, 256), BF16), pl...  53.5 us
    pallas_call x1, Pallas kernels, body(): pl.pallas_call(write_out, out_shape=[jax.ShapeDtypeStruct((32, 16, 16, 25...  2.65 us

profile of v2, /device:TPU:1, one launch (start us, length us, event | category | flops | bytes accessed | tf_op | source)
XLA Modules:
  0.0 56.8 jit_solution(8839619599912238740)
XLA Ops:
  0.6 53.5 %shard_map.110 = (bf16[16,32,16,256]{3,2,1,0:T(8,128)(2,1)S(1)}, bf16[32,96,128]{2,1,0:T(8,128)(2,1)S(1)}) custom-call(bf16[32,16,16,256]{3,2,1,0:T(8,128)(2,1)} %bitcast.3, s32[1,1024]{1,0:T(1,128)} %bal_hbm.1, bf16[32,8,8,512]{3,2,1,0:T(8,128)(2,1)} %bitcast.4, bf16[256,128]{1,0:T(8,128)(2,1)} %wr_hbm.1, bf16[1152,128]{1,0:T(8,128)(2,1)} %wsp_hbm.1, ...), custom_call_target="tpu_custom_call" | custom-call | tf_op jit(solution)/shard_map/pallas_call | solution.py:449
  54.2 2.7 %shard_map.111 = (bf16[32,16,16,256]{3,2,1,0:T(8,128)(2,1)}, f32[256,128]{1,0:T(8,128)}, f32[1152,128]{1,0:T(8,128)}, f32[128,512]{1,0:T(8,128)}, f32[256,512]{1,0:T(8,128)}) custom-call(bf16[16,32,16,256]{3,2,1,0:T(8,128)(2,1)S(1)} %get-tuple-element.12.out_v, bf16[32,96,128]{2,1,0:T(8,128)(2,1)S(1)} %get-tuple-element.13.done), custom_call_target="tpu_custom_call" | custom-call | tf_op jit(solution)/shard_map/pallas_call | solution.py:522

commit v3 on v2

v3 whole, which is shorter than its diff:
```python
import jax
import jax.numpy as jnp
from jax import lax
from jax.experimental import pallas as pl
from jax.experimental.pallas import tpu as pltpu
from jax.sharding import PartitionSpec as P

MESH = pl.DeviceIdType.MESH
F32 = jnp.float32
BF16 = jnp.bfloat16

ROWS = 16
OUT_ROWS = 8
WIDE = 512
HALF_WIDE = 256
MID = 128
N_XY = 16
N_Z = 8
CHUNKS = (80, 16)


def nn(a, b):
    return lax.dot_general(a, b, (((1,), (0,)), ((), ())), preferred_element_type=F32)


def nt(a, b):
    return lax.dot_general(a, b, (((1,), (1,)), ((), ())), preferred_element_type=F32)


def tn(a, b):
    return lax.dot_general(a, b, (((0,), (0,)), ((), ())), preferred_element_type=F32)


def silu_parts(half, scale=None):
    u = jnp.tanh(half)
    twice = 1.0 + u
    if scale is not None:
        twice = twice * scale
    h = half * twice
    return h, twice + h * (1.0 - u)


def kernel(
    x_hbm, bal_hbm, og_hbm, wr_hbm, wsp_hbm, we_hbm, wsc_hbm,
    out_v, done_a, done_b,
    xin, og, wr, wsp, we, wsc, bal,
    mask_in, mask_out, hid, dpre, even, odd, skip_fs, skip, gated, gt, ga2, ga_fs, wb, dacts,
    spreads, gp, zskips, wr_h, wsp_h, we_h, wsc_h,
    acc_a, acc_b, core_a, core_b, xy_out_a, xy_out_b, xy_in_a, xy_in_b, z_in_a, z_in_b,
    x_sem, og_sem, w_sem, halo_send, halo_recv,
    c_send, c_recv, xy_send_a, xy_send_b, xy_recv_a, xy_recv_b,
    z_send_a, z_send_b, z_recv_a, z_recv_b, b_send_a, b_send_b, b_recv_a, b_recv_b,
    f_send_a, f_send_b, f_recv_a, f_recv_b,
):
    s = lax.axis_index("slide")
    t = lax.axis_index("tile")
    y_lo = t // 16
    zi = (t // 2) % N_Z
    core = t % 2
    me = s * 2 + y_lo

    def xy_peer(q):
        return (q // 2, (q % 2) * 16 + t % 16)

    def z_peer(q):
        return (s, y_lo * 16 + q * 2 + core)

    x, y = me // 4, me % 4
    steps = sorted(((a, b) for a in range(4) for b in range(4) if a or b), key=lambda d: -min(d[0], 4 - d[0]) - min(d[1], 4 - d[1]))
    xy_to = [(x + a) % 4 * 4 + (y + b) % 4 for a, b in steps]
    xy_from = [(x + 4 - a) % 4 * 4 + (y + 4 - b) % 4 for a, b in steps]
    z_to = [(zi + k) % N_Z for k in (4, 3, 5, 2, 6, 1, 7)]
    z_from = [(zi + N_Z - k) % N_Z for k in (4, 3, 5, 2, 6, 1, 7)]

    core_peer = (s, t + 1 - 2 * core)
    down = (s, (t + 1) % 32)
    up = (s, (t + 31) % 32)

    def x_copy(y):
        return pltpu.make_async_copy(x_hbm.at[:, y], xin.at[y], x_sem.at[y])

    def og_copy(i):
        return pltpu.make_async_copy(og_hbm.at[:, i], og.at[i], og_sem.at[i])

    w_copies = [
        pltpu.make_async_copy(a, b, w_sem.at[k])
        for k, (a, b) in enumerate(
            [(bal_hbm, bal), (wr_hbm, wr), (wsp_hbm, wsp), (we_hbm, we), (wsc_hbm, wsc)]
        )
    ]
    w_copies[0].start()
    w_copies[1].start()
    x_copy(14).start()
    x_copy(15).start()

    def start_x(y, c):
        x_copy(y).start()
        return c

    lax.fori_loop(0, ROWS - 2, start_x, 0)
    for copy in w_copies[2:]:
        copy.start()

    def start_og(i, c):
        og_copy(i).start()
        return c

    lax.fori_loop(0, OUT_ROWS, start_og, 0)

    barrier = pltpu.get_barrier_semaphore()

    def greet_xy(k, c):
        pl.semaphore_signal(barrier, 1, device_id=xy_peer((me + k) % N_XY), device_id_type=MESH)
        return c

    def greet_z(k, c):
        pl.semaphore_signal(barrier, 1, device_id=z_peer((zi + k) % N_Z), device_id_type=MESH)
        return c

    lax.fori_loop(1, N_XY, greet_xy, 0)
    lax.fori_loop(1, N_Z, greet_z, 0)
    for peer in (core_peer, down, up):
        pl.semaphore_signal(barrier, 1, device_id=peer, device_id_type=MESH)

    w_copies[0].wait()
    window = bal[:, pl.ds(pl.multiple_of((t // 4) * 128, 128), 128)]
    kept = jnp.broadcast_to(jnp.where(window >= 0, 1.0, 0.0).astype(F32), (128, 128)).astype(BF16)
    for ref, side, scale in ((mask_in, 16, 1.0), (mask_out, 8, 0.5)):
        shape = ref.shape
        pixel = lax.broadcasted_iota(jnp.int32, shape, 0) // side
        lane = lax.broadcasted_iota(jnp.int32, shape, 1)
        chosen = jnp.where(lane == (t % 4) * 32 + pixel, 1.0, 0.0).astype(BF16)
        ref[...] = nt(chosen, kept) * scale
    for slot in range(2):
        hid[slot, 0:8] = jnp.zeros((8, MID), F32)
    for ref in ga_fs:
        ref[HALF_WIDE : HALF_WIDE + 8] = jnp.zeros((8, MID), F32)
    acc_b[384:512] = jnp.zeros((128, 128), F32)
    for ref in zskips:
        ref[...] = jnp.zeros(ref.shape, F32)
    w_copies[1].wait()
    wr_h[...] = wr[...] * jnp.asarray(0.5, BF16)

    halo_down = pltpu.make_async_remote_copy(
        odd.at[8], odd.at[0], halo_send.at[0], halo_recv.at[0], device_id=down, device_id_type=MESH
    )
    halo_up = pltpu.make_async_remote_copy(
        ga2.at[0], ga2.at[8], halo_send.at[1], halo_recv.at[1], device_id=up, device_id_type=MESH
    )

    def hidden_pair(k, c):
        i = (k + 7) % 8
        for p in range(2):
            y = 2 * i + p
            x_copy(y).wait()
            for at in range(0, WIDE, 256):
                cols = slice(at, at + 256)
                x = xin[y, at // 16 : (at + 256) // 16].reshape(256, 256)
                h, slope = silu_parts(nn(x, wr_h[...]), mask_in[cols])
                dpre[y, cols] = slope
                hid[p, 8 + at : 8 + at + 256] = h
            target = odd.at[i + 1] if p else even.at[i]
            for v in range(3):
                target[:, v * MID : (v + 1) * MID] = hid[p, pl.ds(7 + v, HALF_WIDE, stride=2)].astype(BF16)

        return c

    lax.fori_loop(0, 8, hidden_pair, 0)
    pl.semaphore_wait(barrier, N_XY - 1 + N_Z - 1 + 3)
    halo_down.start()

    for copy in w_copies[2:]:
        copy.wait()
    for to, of in ((wsp_h, wsp), (we_h, we), (wsc_h, wsc)):
        to[...] = of[...] * jnp.asarray(0.5, BF16)
    for u in range(3):
        tap = u * 3 * MID
        wb[u, 0:MID, 0:MID] = wsp_h[tap + MID : tap + 2 * MID]
        wb[u, 0:MID, MID:] = jnp.zeros((MID, MID), BF16)
        wb[u, MID:, 0:MID] = wsp_h[tap + 2 * MID : tap + 3 * MID]
        wb[u, MID:, MID:] = wsp_h[tap : tap + MID]

    def every_og(i, c):
        og_copy(i).wait()
        return c

    lax.fori_loop(0, 8, every_og, 0)

    def first_stage(n, i):
        half = nn(even[i], wsp_h[384:768]) + nn(odd[i + 1], wsp_h[768:1152]) + nn(odd[i], wsp_h[0:384])
        h, dact = silu_parts(half)
        dacts[n % 3][...] = dact
        gated[i] = h.astype(BF16)
        row = xin[2 * i].reshape(WIDE, 256).astype(F32)
        for side in range(2):
            skip_fs[n % 2][side] = row[:, side * 128 : (side + 1) * 128]
        for side in range(2):
            skip[i, :, side * 128 : (side + 1) * 128] = skip_fs[n % 2][side, pl.ds(0, HALF_WIDE, stride=2)].astype(BF16)

    def second_stage(n, i):
        for row in range(0, HALF_WIDE, 256):
            rows = slice(row, row + 256)
            m = mask_out[rows]
            m = jnp.concatenate([m] * 2, axis=1)
            for col in range(0, 512, 256):
                at = slice(col, col + 256)
                half = nn(gated[i, rows], we_h[:, at]) + nn(skip[i, rows], wsc_h[:, at])
                _, slope = silu_parts(half, m)
                grad = og[i, row // 8 : (row + 256) // 8, :, at].astype(F32).reshape(256, 256)
                gt[i, rows, at] = (grad * slope).astype(BF16)

    def fourth_stage(n, i):
        ga = nt(gt[i], we_h[...]) * dacts[n % 3][...]
        ga2[i, :, 0:MID] = ga.astype(BF16)
        ga_fs[n % 2][0:HALF_WIDE] = ga
        ga2[i, :, MID:] = ga_fs[n % 2][1 : 1 + HALF_WIDE].astype(BF16)

    order = (1, 2, 3, 4, 5, 6, 7, 0)
    for step in range(9):
        if step == 7:
            halo_down.wait_recv()
            odd[0] = odd[0] * jnp.where(t == 0, 0.0, 1.0).astype(BF16)
        if step > 0:
            second_stage(step - 1, order[step - 1])
        if step < 8:
            first_stage(step, order[step])
        if step > 0:
            fourth_stage(step - 1, order[step - 1])
    halo_up.start()

    gt_all = gt[...].reshape(8 * HALF_WIDE, 512)
    part = tn(skip[...].reshape(8 * HALF_WIDE, 256), gt_all)
    for k in range(4):
        acc_a[k * 256 : (k + 1) * 256] = part[:, k * 128 : (k + 1) * 128]
    part = tn(gated[...].reshape(8 * HALF_WIDE, MID), gt_all)
    for k in range(4):
        acc_a[1024 + k * 128 : 1152 + k * 128] = part[:, k * 128 : (k + 1) * 128]
    ga_all = ga2[0:8, :, 0:MID].reshape(8 * HALF_WIDE, MID)
    for u in range(3):
        taps = (odd[0:8], even[...], odd[1:9])[u].reshape(8 * HALF_WIDE, 384)
        part = tn(ga_all, taps)
        for v in range(3):
            tap = u * 3 + v
            to, at = (acc_a, 1536 + tap * 128) if tap < 8 else (acc_b, 0)
            to[at : at + 128] = part[:, v * 128 : (v + 1) * 128]

    def hidden_grad(n, i):
        this = ga2[i]
        for p in range(2):
            if p == 0:
                both = nt(this, wb[1])
            else:
                both = nt(this, wb[2]) + nt(ga2[i + 1], wb[0])
            spreads[n % 2][p, pl.ds(0, HALF_WIDE, stride=2)] = both[:, 0:MID]
            spreads[n % 2][p, pl.ds(1, HALF_WIDE, stride=2)] = both[:, MID:]

    def grad_pair(n, i):
        for p in range(2):
            gp[2 * i + p] = (spreads[n % 2][p] * dpre[2 * i + p]).astype(BF16)

    def grad_pairs(first, last):
        for i in range(first, last + 1):
            if i < last:
                hidden_grad(i, i)
            if i > first:
                grad_pair(i - 1, i - 1)

    def reduce_pairs(first, last):
        rows = (last - first) * 2 * WIDE
        return tn(
            gp[2 * first : 2 * last].reshape(rows, MID), xin[2 * first : 2 * last].reshape(rows, 256)
        )

    def out_pair(i):
        back = nt(gt[i], wsc[...])
        for half in range(2):
            zskips[i % 2][half, pl.ds(0, HALF_WIDE, stride=2)] = back[:, half * 128 : (half + 1) * 128]
        first = nt(gp[2 * i], wr[...]) + jnp.concatenate([zskips[i % 2][0], zskips[i % 2][1]], axis=1)
        out_v[2 * i] = first.astype(BF16).reshape(32, 16, 256)
        second = nt(gp[2 * i + 1], wr[...])
        out_v[2 * i + 1] = second.astype(BF16).reshape(32, 16, 256)

    accs, cores = (acc_a, acc_b), (core_a, core_b)
    xy_outs, xy_ins = (xy_out_a, xy_out_b), (xy_in_a, xy_in_b)
    xy_sends, xy_recvs = (xy_send_a, xy_send_b), (xy_recv_a, xy_recv_b)
    z_ins, dones = (z_in_a, z_in_b), (done_a, done_b)
    z_sends, z_recvs = (z_send_a, z_send_b), (z_recv_a, z_recv_b)
    b_sends, b_recvs = (b_send_a, b_send_b), (b_recv_a, b_recv_b)
    f_sends, f_recvs = (f_send_a, f_send_b), (f_recv_a, f_recv_b)

    def core_copy(part):
        rows = N_XY * CHUNKS[part]
        return pltpu.make_async_remote_copy(
            accs[part].at[pl.ds(pl.multiple_of((1 - core) * rows, 8), rows)], cores[part],
            c_send.at[part], c_recv.at[part], device_id=core_peer, device_id_type=MESH,
        )

    def xy_copy(part, q, slot):
        return pltpu.make_async_remote_copy(
            xy_outs[part].at[q], xy_ins[part].at[slot], xy_sends[part].at[q], xy_recvs[part].at[slot],
            device_id=xy_peer(q), device_id_type=MESH,
        )

    def both_cores(part, q):
        chunk = CHUNKS[part]
        at = pl.multiple_of(q * chunk, 8)
        kept = accs[part][pl.ds(pl.multiple_of(core * (N_XY * chunk) + at, 8), chunk)]
        return kept + cores[part][pl.ds(at, chunk)]

    def send_xy(part):
        for q in xy_to:
            xy_outs[part][q] = both_cores(part, q).astype(BF16)
            xy_copy(part, q, me).start()

    def take_xy(part):
        total = both_cores(part, me)
        for q in xy_from:
            xy_copy(part, q, q).wait_recv()
            total = total + xy_ins[part][q].astype(F32)
        return total

    def z_copy(part, q, slot):
        return pltpu.make_async_remote_copy(
            z_ins[part].at[zi], z_ins[part].at[slot], z_sends[part].at[q], z_recvs[part].at[slot],
            device_id=z_peer(q), device_id_type=MESH,
        )

    def send_z(part):
        z_ins[part][zi] = take_xy(part).astype(BF16)

        for q in z_to:
            z_copy(part, q, zi).start()

    mine = core * N_XY

    def back_copy(part, q, slot):
        return pltpu.make_async_remote_copy(
            dones[part].at[mine + me], dones[part].at[mine + slot], b_sends[part].at[q], b_recvs[part].at[slot],
            device_id=xy_peer(q), device_id_type=MESH,
        )

    def pass_copy(part, q, side):
        return pltpu.make_async_remote_copy(
            dones[part].at[mine + q], dones[part].at[side * N_XY + q], f_sends[part].at[q], f_recvs[part].at[q],
            device_id=core_peer, device_id_type=MESH,
        )

    def send_back(part):
        for q in z_from:
            z_copy(part, q, q).wait_recv()
        whole = z_ins[part][0].astype(F32)
        for q in range(1, N_Z):
            whole = whole + z_ins[part][q].astype(F32)
        dones[part][mine + me] = whole.astype(BF16)

        for q in xy_to:
            back_copy(part, q, me).start()
        pass_copy(part, me, core).start()

    def pass_on(part):
        for q in xy_from:
            back_copy(part, q, q).wait_recv()
            pass_copy(part, q, core).start()

    core_copy(0).start()
    grad_pairs(0, 2)
    core_copy(0).wait_recv()
    send_xy(0)
    halo_up.wait_recv()
    ga2[8] = ga2[8] * jnp.where(t == 31, 0.0, 1.0).astype(BF16)
    grad_pairs(2, 8)
    total = reduce_pairs(0, 8)
    acc_b[128:256] = total[:, 0:128]
    acc_b[256:384] = total[:, 128:256]
    core_copy(1).start()
    for i in range(0, 2):
        out_pair(i)
    core_copy(1).wait_recv()
    send_xy(1)
    send_z(0)
    for i in range(2, 6):
        out_pair(i)
    send_z(1)
    for i in range(6, 8):
        out_pair(i)
    send_back(0)
    send_back(1)
    pass_on(0)
    pass_on(1)

    halo_down.wait_send()
    halo_up.wait_send()
    for part in range(2):
        core_copy(part).wait_send()

    def sent_xy(k, c):
        q = (me + k) % N_XY
        for part in range(2):
            xy_copy(part, q, me).wait_send()
            back_copy(part, q, me).wait_send()
        return c

    lax.fori_loop(1, N_XY, sent_xy, 0)

    def sent_z(k, c):
        for part in range(2):
            z_copy(part, (zi + k) % N_Z, zi).wait_send()
        return c

    lax.fori_loop(1, N_Z, sent_z, 0)

    def passed(k, c):
        q = (me + N_XY - k) % N_XY
        for part in range(2):
            pass_copy(part, q, core).wait_send()
            pass_copy(part, q, 1 - core).wait_recv()
        return c

    lax.fori_loop(0, N_XY, passed, 0)


def write_out(
    out_v, done_a, done_b, ig_hbm, gr_hbm, gsp_hbm, gexp_hbm, gsc_hbm, gr, gsp, gexp, gsc, out_sem, w_sem
):
    copies = [
        pltpu.make_async_copy(out_v.at[y], ig_hbm.at[:, y], out_sem.at[y]) for y in range(ROWS)
    ]
    for copy in copies:
        copy.start()
    part = done_a[...].astype(F32).reshape(2560, 128)
    last = done_b[...].astype(F32).reshape(512, 128)
    for k in range(4):
        gsc[:, k * 128 : (k + 1) * 128] = part[k * 256 : (k + 1) * 256]
        gexp[:, k * 128 : (k + 1) * 128] = part[1024 + k * 128 : 1152 + k * 128]
    for k in range(8):
        gsp[k * 128 : (k + 1) * 128] = part[1536 + k * 128 : 1664 + k * 128].T
    gsp[1024:1152] = last[0:128].T
    for k in range(2):
        gr[k * 128 : (k + 1) * 128] = last[128 + k * 128 : 256 + k * 128].T
    pairs = ((gr, gr_hbm), (gsp, gsp_hbm), (gexp, gexp_hbm), (gsc, gsc_hbm))
    more = [pltpu.make_async_copy(a, b, w_sem.at[k]) for k, (a, b) in enumerate(pairs)]
    for copy in more:
        copy.start()
    for copy in copies + more:
        copy.wait()


def body(slide_tiles, balance_list, output_grad, w_reduce, w_spatial, w_expand, w_shortcut):
    dma = pltpu.SemaphoreType.DMA
    any_spec = pl.BlockSpec(memory_space=pltpu.HBM)
    vmem_spec = pl.BlockSpec(memory_space=pltpu.VMEM)
    out_v, done_a, done_b = pl.pallas_call(
        kernel,
        out_shape=(
            pltpu.VMEM((16, 32, 16, 256), BF16),
            pltpu.VMEM((2 * N_XY, CHUNKS[0], 128), BF16),
            pltpu.VMEM((2 * N_XY, CHUNKS[1], 128), BF16),
        ),
        in_specs=[any_spec] * 7,
        out_specs=(vmem_spec, vmem_spec, vmem_spec),
        scratch_shapes=[
            pltpu.VMEM((16, 32, 16, 256), BF16),
            pltpu.VMEM((8, 32, 8, 512), BF16),
            pltpu.VMEM((256, 128), BF16),
            pltpu.VMEM((1152, 128), BF16),
            pltpu.VMEM((128, 512), BF16),
            pltpu.VMEM((256, 512), BF16),
            pltpu.VMEM((1, 1024), jnp.int32),
            pltpu.VMEM((WIDE, 128), F32),
            pltpu.VMEM((HALF_WIDE, 128), F32),
            pltpu.VMEM((2, WIDE + 16, MID), F32),
            pltpu.VMEM((16, WIDE, MID), F32),
            pltpu.VMEM((8, HALF_WIDE, 384), BF16),
            pltpu.VMEM((9, HALF_WIDE, 384), BF16),
            [pltpu.VMEM((2, WIDE, 128), F32)] * 2,
            pltpu.VMEM((8, HALF_WIDE, 256), BF16),
            pltpu.VMEM((8, HALF_WIDE, MID), BF16),
            pltpu.VMEM((8, HALF_WIDE, 512), BF16),
            pltpu.VMEM((9, HALF_WIDE, 256), BF16),
            [pltpu.VMEM((HALF_WIDE + 8, MID), F32)] * 2,
            pltpu.VMEM((3, 256, 256), BF16),
            [pltpu.VMEM((HALF_WIDE, MID), F32)] * 3,
            [pltpu.VMEM((2, WIDE, MID), F32)] * 2,
            pltpu.VMEM((16, WIDE, MID), BF16),
            [pltpu.VMEM((2, WIDE, 128), F32)] * 2,
            pltpu.VMEM((256, 128), BF16),
            pltpu.VMEM((1152, 128), BF16),
            pltpu.VMEM((128, 512), BF16),
            pltpu.VMEM((256, 512), BF16),
            pltpu.VMEM((2560, 128), F32),
            pltpu.VMEM((512, 128), F32),
            pltpu.VMEM((1280, 128), F32),
            pltpu.VMEM((256, 128), F32),
            pltpu.VMEM((N_XY, 80, 128), BF16),
            pltpu.VMEM((N_XY, 16, 128), BF16),
            pltpu.VMEM((N_XY, 80, 128), BF16),
            pltpu.VMEM((N_XY, 16, 128), BF16),
            pltpu.VMEM((N_Z, 80, 128), BF16),
            pltpu.VMEM((N_Z, 16, 128), BF16),
            dma((16,)),
            dma((8,)),
            dma((5,)),
            dma((2,)),
            dma((2,)),
            dma((2,)),
            dma((2,)),
            *[dma((N_XY,))] * 4,
            *[dma((N_Z,))] * 4,
            *[dma((N_XY,))] * 8,
        ],
        compiler_params=pltpu.CompilerParams(
            collective_id=0, has_side_effects=True, vmem_limit_bytes=59 * 2**20
        ),
    )(slide_tiles[0], balance_list, output_grad[0], w_reduce, w_spatial, w_expand, w_shortcut)
    shapes = ((256, 128), (1152, 128), (128, 512), (256, 512))
    out = pl.pallas_call(
        write_out,
        out_shape=[jax.ShapeDtypeStruct((32, 16, 16, 256), BF16)]
        + [jax.ShapeDtypeStruct(shape, F32) for shape in shapes],
        in_specs=[vmem_spec] * 3,
        out_specs=[any_spec] * 5,
        scratch_shapes=[pltpu.VMEM(shape, F32) for shape in shapes] + [dma((16,)), dma((4,))],
        compiler_params=pltpu.CompilerParams(vmem_limit_bytes=16 * 2**20),
    )(out_v, done_a, done_b)
    return (out[0][None], out[1], out[2], out[3], out[4])


def solution(mesh):
    in_specs = (
        P("slide", "tile", None, None, None),
        P("slide", None),
        P("slide", "tile", None, None, None),
        P(),
        P(),
        P(),
        P(),
    )
    out_specs = (P("slide", "tile", None, None, None), P(), P(), P(), P())
    return jax.shard_map(body, mesh=mesh, in_specs=in_specs, out_specs=out_specs, check_vma=False)
```

time: 56.9 us -> 48.7 us (0.86)
  Pallas kernels: 56.2 us -> 48 us
    pallas_call x1, Pallas kernels: 53.5 us -> 45.3 us  [body(): pl.pallas_call(kernel, out_shape=(pltpu.VMEM((16, 32, 16, 256), BF16), pl...]
where the time goes in v3:
time: 48.7 us; the launch traced here: 48.6 us
  Pallas kernels  48 us (99%)
  between operations  0.64 us (1%)
    pallas_call x1, Pallas kernels, body(): pl.pallas_call(kernel, out_shape=(pltpu.VMEM((16, 32, 16, 256), BF16), pl...  45.3 us
    pallas_call x1, Pallas kernels, body(): pl.pallas_call(write_out, out_shape=[jax.ShapeDtypeStruct((32, 16, 16, 25...  2.73 us

profile of v3, /device:TPU:1, one launch (start us, length us, event | category | flops | bytes accessed | tf_op | source)
XLA Modules:
  0.0 48.6 jit_solution(15455291273080013977)
XLA Ops:
  0.6 45.3 %shard_map.110 = (bf16[16,32,16,256]{3,2,1,0:T(8,128)(2,1)S(1)}, bf16[32,80,128]{2,1,0:T(8,128)(2,1)S(1)}, bf16[32,16,128]{2,1,0:T(8,128)(2,1)S(1)}) custom-call(bf16[32,16,16,256]{3,2,1,0:T(8,128)(2,1)} %bitcast.3, s32[1,1024]{1,0:T(1,128)} %bal_hbm.1, bf16[32,8,8,512]{3,2,1,0:T(8,128)(2,1)} %bitcast.4, bf16[256,128]{1,0:T(8,128)(2,1)} %wr_hbm.1, ...), custom_call_target="tpu_custom_call" | custom-call | tf_op jit(solution)/shard_map/pallas_call | solution.py:452
  45.9 2.7 %shard_map.111 = (bf16[32,16,16,256]{3,2,1,0:T(8,128)(2,1)}, f32[256,128]{1,0:T(8,128)}, f32[1152,128]{1,0:T(8,128)}, f32[128,512]{1,0:T(8,128)}, f32[256,512]{1,0:T(8,128)}) custom-call(bf16[16,32,16,256]{3,2,1,0:T(8,128)(2,1)S(1)} %get-tuple-element.13.out_v, bf16[32,80,128]{2,1,0:T(8,128)(2,1)S(1)} %get-tuple-element.14.done_a, ...), custom_call_target="tpu_custom_call" | custom-call | tf_op jit(solution)/shard_map/pallas_call | solution.py:516

commit v4 on v3

--- a/solution.py
+++ b/solution.py
@@ -276,9 +276,9 @@
         for half in range(2):
             zskips[i % 2][half, pl.ds(0, HALF_WIDE, stride=2)] = back[:, half * 128 : (half + 1) * 128]
         first = nt(gp[2 * i], wr[...]) + jnp.concatenate([zskips[i % 2][0], zskips[i % 2][1]], axis=1)
-        out_v[2 * i] = first.astype(BF16).reshape(32, 16, 256)
+        out_v[:, 2 * i] = first.astype(BF16).reshape(32, 16, 256)
         second = nt(gp[2 * i + 1], wr[...])
-        out_v[2 * i + 1] = second.astype(BF16).reshape(32, 16, 256)
+        out_v[:, 2 * i + 1] = second.astype(BF16).reshape(32, 16, 256)
 
     accs, cores = (acc_a, acc_b), (core_a, core_b)
     xy_outs, xy_ins = (xy_out_a, xy_out_b), (xy_in_a, xy_in_b)
@@ -423,7 +423,7 @@
     out_v, done_a, done_b, ig_hbm, gr_hbm, gsp_hbm, gexp_hbm, gsc_hbm, gr, gsp, gexp, gsc, out_sem, w_sem
 ):
     copies = [
-        pltpu.make_async_copy(out_v.at[y], ig_hbm.at[:, y], out_sem.at[y]) for y in range(ROWS)
+        pltpu.make_async_copy(out_v.at[8 * k : 8 * k + 8], ig_hbm.at[8 * k : 8 * k + 8], out_sem.at[k]) for k in range(4)
     ]
     for copy in copies:
         copy.start()
@@ -452,7 +452,7 @@
     out_v, done_a, done_b = pl.pallas_call(
         kernel,
         out_shape=(
-            pltpu.VMEM((16, 32, 16, 256), BF16),
+            pltpu.VMEM((32, 16, 16, 256), BF16),
             pltpu.VMEM((2 * N_XY, CHUNKS[0], 128), BF16),
             pltpu.VMEM((2 * N_XY, CHUNKS[1], 128), BF16),
         ),
@@ -519,7 +519,7 @@
         + [jax.ShapeDtypeStruct(shape, F32) for shape in shapes],
         in_specs=[vmem_spec] * 3,
         out_specs=[any_spec] * 5,
-        scratch_shapes=[pltpu.VMEM(shape, F32) for shape in shapes] + [dma((16,)), dma((4,))],
+        scratch_shapes=[pltpu.VMEM(shape, F32) for shape in shapes] + [dma((4,)), dma((4,))],
         compiler_params=pltpu.CompilerParams(vmem_limit_bytes=16 * 2**20),
     )(out_v, done_a, done_b)
     return (out[0][None], out[1], out[2], out[3], out[4])

time: 48.7 us -> 48.5 us (level)
  no operation moved by 1% of the time
where the time goes in v4:
time: 48.5 us; the launch traced here: 48.4 us
  Pallas kernels  47.8 us (99%)
  between operations  0.64 us (1%)
    pallas_call x1, Pallas kernels, body(): pl.pallas_call(kernel, out_shape=(pltpu.VMEM((32, 16, 16, 256), BF16), pl...  45.3 us
    pallas_call x1, Pallas kernels, body(): pl.pallas_call(write_out, out_shape=[jax.ShapeDtypeStruct((32, 16, 16, 25...  2.54 us

profile of v4, /device:TPU:1, one launch (start us, length us, event | category | flops | bytes accessed | tf_op | source)
XLA Modules:
  0.0 48.4 jit_solution(15130996541381087611)
XLA Ops:
  0.6 45.3 %shard_map.110 = (bf16[32,16,16,256]{3,2,1,0:T(8,128)(2,1)S(1)}, bf16[32,80,128]{2,1,0:T(8,128)(2,1)S(1)}, bf16[32,16,128]{2,1,0:T(8,128)(2,1)S(1)}) custom-call(bf16[32,16,16,256]{3,2,1,0:T(8,128)(2,1)} %bitcast.3, s32[1,1024]{1,0:T(1,128)} %bal_hbm.1, bf16[32,8,8,512]{3,2,1,0:T(8,128)(2,1)} %bitcast.4, bf16[256,128]{1,0:T(8,128)(2,1)} %wr_hbm.1, ...), custom_call_target="tpu_custom_call" | custom-call | tf_op jit(solution)/shard_map/pallas_call | solution.py:452
  45.9 2.5 %shard_map.111 = (bf16[32,16,16,256]{3,2,1,0:T(8,128)(2,1)}, f32[256,128]{1,0:T(8,128)}, f32[1152,128]{1,0:T(8,128)}, f32[128,512]{1,0:T(8,128)}, f32[256,512]{1,0:T(8,128)}) custom-call(bf16[32,16,16,256]{3,2,1,0:T(8,128)(2,1)S(1)} %get-tuple-element.13.out_v, bf16[32,80,128]{2,1,0:T(8,128)(2,1)S(1)} %get-tuple-element.14.done_a, ...), custom_call_target="tpu_custom_call" | custom-call | tf_op jit(solution)/shard_map/pallas_call | solution.py:516
